TPU v7x, 512 devices: a whole 4x8x8 slice. The times are simulated.
512 devices in a mesh: fsdp: 16 (over y_lo, x, core), ctx: 32 (over y_hi, z).
Axes of the slice: x: 4, y: 8 (y_hi: 4, y_lo: 2; y = y_hi * 2 + y_lo), z: 8, core: 2. Of those that a mesh axis runs over, the one named last changes fastest.
Arguments:
- queries: bfloat16 [16, 4096, 1024], P('fsdp', 'ctx'), may hold values from -6 to 6
- keys: bfloat16 [16, 4096, 1024], P('fsdp', 'ctx'), may hold values from -8 to 8
- values: bfloat16 [16, 4096, 1024], P('fsdp', 'ctx'), may hold values from -6 to 6
- out_grad: bfloat16 [16, 4096, 2048], P('fsdp', 'ctx'), may hold values from -6 to 6
- weight: bfloat16 [2048, 1024], P('fsdp'), may hold values from -0.1875 to 0.1875
- neighbours: int32 [16, 32, 4], P('fsdp'), may hold values from -1 to 31, as said below
Outputs:
- outputs: bfloat16 [16, 4096, 2048], P('fsdp', 'ctx')
- query_grad: bfloat16 [16, 4096, 1024], P('fsdp', 'ctx')
- key_grad: bfloat16 [16, 4096, 1024], P('fsdp', 'ctx')
- value_grad: bfloat16 [16, 4096, 1024], P('fsdp', 'ctx')
- weight_grad: float32 [2048, 1024], P('fsdp')
Inputs may be any that keep to these rules, and one draw needn't show every extreme that they name: `neighbours`: slot 0 of block j is j itself. Each other live slot names a block b with b // 1 at cycle distance 1 to 2 from j // 1 along 32 // 1 positions (cyclic), distinct live slots of one row lying at distinct distances with sign; live slots come first, then -1 padding; slot 1 is always live.
All inputs are finite; a program needn't handle non-finite values.
Results may differ from a plain program's by a relative error of at most 0.034.
Values may be sent and summed in bfloat16 or wider, within the bound.
A program may use at most 64 MiB of HBM per device.

v0:
```python
import math

import jax
import jax.numpy as jnp
from jax import lax
from jax.sharding import PartitionSpec as P

HEADS = 8
HDIM = 128
BS = 128
NB = 4
HOPS = 2


def shifted(block, axis, distance):
    devices = range(lax.axis_size(axis))
    route = [((i - distance) % len(devices), i) for i in devices]
    return lax.ppermute(block, axis, route)


def window_slots(slot_blocks, centre, cycle_size, per_dev, far_reach):
    safe_blocks = jnp.where(slot_blocks >= 0, slot_blocks, 0)
    offset = (safe_blocks // per_dev - centre) % cycle_size
    offset = jnp.where(offset > far_reach, offset - cycle_size, offset)
    return (offset + far_reach) * per_dev + safe_blocks % per_dev


def fetch_direct(packed, shift_by):
    return shifted(packed, "ctx", shift_by)


def send_back(partial_grads, shift_by):
    return shifted(partial_grads, "ctx", shift_by)


def body(queries, keys, values, out_grad, weight, neighbours):
    cycle_size = lax.axis_size("ctx")
    centre = lax.axis_index("ctx")
    far_reach = HOPS
    head_count = HEADS
    head_size = HDIM
    block_rows = BS
    slot_count = NB
    token_count = queries.shape[1]
    feature_width = queries.shape[2]
    model_width = out_grad.shape[2]
    per_dev = token_count // block_rows
    score_scale = head_size ** (-0.5)
    query_rows = queries[0]
    key_rows = keys[0]
    value_rows = values[0]
    grad_rows = out_grad[0]
    packed = jnp.concatenate([key_rows, value_rows], axis=1)
    window_parts = [
        packed if offset == 0 else fetch_direct(packed, -offset)
        for offset in range(-far_reach, far_reach + 1)
    ]
    window = jnp.stack(window_parts)
    local_slots = lax.dynamic_slice_in_dim(neighbours[0], centre * per_dev, per_dev, 0)
    slot_live = local_slots >= 0
    slot_index = window_slots(local_slots, centre, cycle_size, per_dev, far_reach)
    chosen = window[slot_index]
    key_sel = chosen[..., :feature_width].reshape(
        per_dev, slot_count, block_rows, head_count, head_size
    )
    value_sel = chosen[..., feature_width:].reshape(
        per_dev, slot_count, block_rows, head_count, head_size
    )
    query_heads = query_rows.reshape(per_dev, block_rows, head_count, head_size)
    scores = (
        jnp.einsum("bqhd,bnkhd->bhqnk", query_heads, key_sel, preferred_element_type=jnp.float32)
        * score_scale
    )
    scores = jnp.where(slot_live[:, None, None, :, None], scores, -jnp.inf)
    row_max = jnp.max(scores, axis=(3, 4), keepdims=True)
    row_sum = jnp.sum(jnp.exp(scores - row_max), axis=(3, 4), keepdims=True)
    log_total = row_max + jnp.log(row_sum)
    probs_full = jnp.exp(scores - log_total)
    probs_half = probs_full.astype(jnp.bfloat16)
    attended = jnp.einsum(
        "bhqnk,bnkhd->bqhd", probs_half, value_sel, preferred_element_type=jnp.float32
    ).astype(jnp.bfloat16)
    attended_flat = attended.reshape(token_count, feature_width)
    weight_piece = lax.all_gather(weight, "fsdp", axis=0, tiled=True)
    column_block = lax.dot_general(
        attended_flat, weight_piece, (((1,), (1,)), ((), ())), preferred_element_type=jnp.float32
    )
    output_cols = column_block
    grad_cols = grad_rows
    rows_grad = jnp.dot(grad_cols, weight_piece, preferred_element_type=jnp.float32)
    output_cols, rows_grad = (output_cols, rows_grad)
    outputs = output_cols.astype(jnp.bfloat16).reshape(1, token_count, model_width)
    grad_half = rows_grad.astype(jnp.bfloat16)
    grad_heads = grad_half.reshape(per_dev, block_rows, head_count, head_size)
    row_delta = jnp.einsum(
        "bqhd,bqhd->bhq", grad_heads, attended, preferred_element_type=jnp.float32
    )
    prob_grad = jnp.einsum(
        "bqhd,bnkhd->bhqnk", grad_heads, value_sel, preferred_element_type=jnp.float32
    )
    dscore = (probs_full * (prob_grad - row_delta[..., None, None]) * score_scale).astype(
        jnp.bfloat16
    )
    query_grad = jnp.einsum(
        "bhqnk,bnkhd->bqhd", dscore, key_sel, preferred_element_type=jnp.float32
    )
    query_grad = query_grad.astype(jnp.bfloat16).reshape(1, token_count, feature_width)
    key_slot = jnp.einsum(
        "bhqnk,bqhd->bnkhd", dscore, query_heads, preferred_element_type=jnp.float32
    )
    value_slot = jnp.einsum(
        "bhqnk,bqhd->bnkhd", probs_half, grad_heads, preferred_element_type=jnp.float32
    )
    slot_total = per_dev * slot_count
    slot_grads = jnp.concatenate(
        [
            key_slot.reshape(slot_total, block_rows, feature_width),
            value_slot.reshape(slot_total, block_rows, feature_width),
        ],
        axis=2,
    )
    window_count = (2 * far_reach + 1) * per_dev
    placement = ((slot_index == jnp.arange(window_count)[:, None]) & slot_live).astype(jnp.float32)
    window_grads = jnp.dot(
        placement,
        slot_grads.reshape(slot_total, block_rows * 2 * feature_width),
        precision=lax.Precision.HIGHEST,
    )
    window_grads = window_grads.reshape(2 * far_reach + 1, token_count, 2 * feature_width).astype(
        jnp.bfloat16
    )
    owned_grads = window_grads[far_reach].astype(jnp.float32)
    for offset in range(-far_reach, far_reach + 1):
        if offset != 0:
            owned_grads = owned_grads + send_back(window_grads[offset + far_reach], offset).astype(
                jnp.float32
            )
    key_grad = (
        owned_grads[:, :feature_width].astype(jnp.bfloat16).reshape(1, token_count, feature_width)
    )
    value_grad = (
        owned_grads[:, feature_width:].astype(jnp.bfloat16).reshape(1, token_count, feature_width)
    )
    grad_cols = grad_rows
    fsdp_sum = lax.psum_scatter(
        lax.dot_general(
            grad_cols, attended_flat, (((0,), (0,)), ((), ())), preferred_element_type=jnp.float32
        ).astype(jnp.bfloat16),
        "fsdp",
        scatter_dimension=0,
        tiled=True,
    ).astype(jnp.float32)
    full_sum = lax.psum(fsdp_sum, "ctx")
    all_tokens = lax.axis_size("fsdp") * cycle_size * token_count
    weight_grad = full_sum * (1.0 / math.sqrt(all_tokens))
    return (outputs, query_grad, key_grad, value_grad, weight_grad)


def solution(mesh):
    placed = (
        P("fsdp", "ctx", None),
        P("fsdp", "ctx", None),
        P("fsdp", "ctx", None),
        P("fsdp", "ctx", None),
        P("fsdp", None),
        P("fsdp", None, None),
    )
    return jax.shard_map(
        body,
        mesh=mesh,
        in_specs=placed,
        out_specs=(
            P("fsdp", "ctx", None),
            P("fsdp", "ctx", None),
            P("fsdp", "ctx", None),
            P("fsdp", "ctx", None),
            P("fsdp", None),
        ),
        check_vma=False,
    )
```

profile of v0, /device:TPU:8, one launch (start us, length us, event | category | flops | bytes accessed | tf_op | source)
XLA Modules:
  0.0 386.4 jit_solution(14807924794882000671)
XLA Ops:
  8.0 1.1 pad_maximum_fusion.1
  9.1 6.1 %collective-permute-start = (bf16[128,2048]{1,0:T(8,128)(2,1)S(1)}, bf16[128,2048]{1,0:T(8,128)(2,1)}, u32[]{:S(2)}, u32[]{:S(2)}) collective-permute-start(bf16[128,2048]{1,0:T(8,128)(2,1)S(1)} %pad_maximum_fusion.1), channel_id=1, source_target_pairs={{30,0},{31,1},{0,2},{1,3},{2,4},{3,5},{4,6},{5,7},{6,8},{7,9},{8,1... | collective-permute-start | bytes 1572872 | tf_op jit(solution)/shard_map/ppermute | solution.py:18
  15.2 4.3 %collective-permute-start.1 = (bf16[128,2048]{1,0:T(8,128)(2,1)S(1)}, bf16[128,2048]{1,0:T(8,128)(2,1)}, u32[]{:S(2)}, u32[]{:S(2)}) collective-permute-start(bf16[128,2048]{1,0:T(8,128)(2,1)S(1)} %pad_maximum_fusion.1), channel_id=1, source_target_pairs={{31,0},{0,1},{1,2},{2,3},{3,4},{4,5},{5,6},{6,7},{7,8},{8,9},{9,10... | collective-permute-start | bytes 1572872 | tf_op jit(solution)/shard_map/ppermute | solution.py:18
  19.5 7.2 %collective-permute-start.2 = (bf16[128,2048]{1,0:T(8,128)(2,1)S(1)}, bf16[128,2048]{1,0:T(8,128)(2,1)S(1)}, u32[]{:S(2)}, u32[]{:S(2)}) collective-permute-start(bf16[128,2048]{1,0:T(8,128)(2,1)S(1)} %pad_maximum_fusion.1), channel_id=1, source_target_pairs={{1,0},{2,1},{3,2},{4,3},{5,4},{6,5},{7,6},{8,7},{9,8},{10,9},{11,1... | collective-permute-start | bytes 1572872 | tf_op jit(solution)/shard_map/ppermute | solution.py:18
  26.7 4.8 %collective-permute-start.3 = (bf16[128,2048]{1,0:T(8,128)(2,1)S(1)}, bf16[128,2048]{1,0:T(8,128)(2,1)S(1)}, u32[]{:S(2)}, u32[]{:S(2)}) collective-permute-start(bf16[128,2048]{1,0:T(8,128)(2,1)S(1)} %pad_maximum_fusion.1), channel_id=1, source_target_pairs={{2,0},{3,1},{4,2},{5,3},{6,4},{7,5},{8,6},{9,7},{10,8},{11,9},{12,... | collective-permute-start | bytes 1572872 | tf_op jit(solution)/shard_map/ppermute | solution.py:18
  31.5 0.9 dynamic-slice_reduce_fusion
  32.5 1.0 copy.159
  33.7 14.5 %collective-permute-done = bf16[128,2048]{1,0:T(8,128)(2,1)} collective-permute-done((bf16[128,2048]{1,0:T(8,128)(2,1)S(1)}, bf16[128,2048]{1,0:T(8,128)(2,1)}, u32[]{:S(2)}, u32[]{:S(2)}) %collective-permute-start) | collective-permute-done | bytes 524320 | tf_op jit(solution)/shard_map/ppermute | solution.py:18
  48.2 1.9 bitcast_dynamic-update-slice_fusion.4
  50.1 7.8 %collective-permute-done.1 = bf16[128,2048]{1,0:T(8,128)(2,1)} collective-permute-done((bf16[128,2048]{1,0:T(8,128)(2,1)S(1)}, bf16[128,2048]{1,0:T(8,128)(2,1)}, u32[]{:S(2)}, u32[]{:S(2)}) %collective-permute-start.1) | collective-permute-done | bytes 524320 | tf_op jit(solution)/shard_map/ppermute | solution.py:18
  57.9 1.9 bitcast_dynamic-update-slice_fusion.3
  59.8 0.9 bitcast_dynamic-update-slice_fusion.2
  60.7 9.4 %collective-permute-done.2 = bf16[128,2048]{1,0:T(8,128)(2,1)S(1)} collective-permute-done((bf16[128,2048]{1,0:T(8,128)(2,1)S(1)}, bf16[128,2048]{1,0:T(8,128)(2,1)S(1)}, u32[]{:S(2)}, u32[]{:S(2)}) %collective-permute-start.2) | collective-permute-done | bytes 524320 | tf_op jit(solution)/shard_map/ppermute | solution.py:18
  70.9 19.2 %collective-permute-done.3 = bf16[128,2048]{1,0:T(8,128)(2,1)S(1)} collective-permute-done((bf16[128,2048]{1,0:T(8,128)(2,1)S(1)}, bf16[128,2048]{1,0:T(8,128)(2,1)S(1)}, u32[]{:S(2)}, u32[]{:S(2)}) %collective-permute-start.3) | collective-permute-done | bytes 524320 | tf_op jit(solution)/shard_map/ppermute | solution.py:18
  91.0 2.4 gather_fusion
  93.4 1.6 fusion.29
  95.0 2.4 copy.105
  97.4 1.3 copy.106
  98.7 1.8 bitcast_reduce_fusion
  100.8 2.9 fusion.7
  103.8 1.0 copy.134
  104.9 1.9 multiply_reduce_fusion
  106.8 3.2 convert_bitcast_fusion
  110.0 6.4 %copy.152 = bf16[2048,1024]{1,0:T(8,128)(2,1)} copy(bf16[2048,1024]{0,1:T(8,128)(2,1)} %convert_bitcast_fusion) | data formatting | bytes 8388608
  117.3 1.1 copy-done.1
  120.3 2.2 pad_maximum_fusion
  122.5 5.4 %copy.120 = f32[4,128,2048]{2,1,0:T(8,128)} copy(f32[4,128,2048]{1,2,0:T(8,128)} %pad_maximum_fusion) | data formatting | bytes 8388608 | tf_op jit(solution)/shard_map/concatenate | solution.py:115
  127.9 10.0 %convolution_convert_fusion = bf16[5,128,2048]{2,0,1:T(8,128)(2,1)S(1)} fusion(s32[4]{0:T(128)S(1)} %fusion.27, pred[4]{0:T(512)(128)(4,1)S(1)} %broadcast_compare_fusion, f32[1,4,128,2048]{3,2,1,0:T(8,128)} %bitcast.149), kind=kOutput, calls=%fused_computation.3 | convolution fusion | flops 64225320 | bytes 6815764 | tf_op jit(solution)/shard_map/dot_general | solution.py:124
  137.9 4.1 %fusion.28 = (bf16[1,128,2048]{2,0,1:T(2,128)(2,1)S(1)}, bf16[1,128,2048]{2,0,1:T(2,128)(2,1)S(1)}, bf16[1,128,2048]{2,0,1:T(2,128)(2,1)S(1)}, bf16[1,128,2048]{2,0,1:T(2,128)(2,1)S(1)}, f32[1,128,2048]{2,0,1:T(1,128)S(1)}) fusion(bf16[5,128,2048]{2,0,1:T(8,128)(2,1)S(1)} %convolution_convert_fusion), kind=kLoop, calls=%fused_computation.74 | loop fusion | flops 262144 | bytes 5767168 | tf_op jit(solution)/shard_map/slice | solution.py:135
  142.0 1.1 copy.183
  143.1 1.9 collective-permute-start.7
  145.0 1.1 copy.184
  146.1 1.9 collective-permute-start.6
  148.1 1.1 copy.185
  149.2 8.1 %collective-permute-start.5 = (bf16[128,2048]{1,0:T(8,128)(2,1)}, bf16[128,2048]{1,0:T(8,128)(2,1)}, u32[]{:S(2)}, u32[]{:S(2)}) collective-permute-start(bf16[128,2048]{1,0:T(8,128)(2,1)} %bitcast.147), channel_id=1, source_target_pairs={{1,0},{2,1},{3,2},{4,3},{5,4},{6,5},{7,6},{8,7},{9,8},{10,9},{11,1... | collective-permute-start | bytes 1572872 | tf_op jit(solution)/shard_map/ppermute | solution.py:18
  157.3 1.1 copy.186
  158.4 5.4 %collective-permute-start.4 = (bf16[128,2048]{1,0:T(8,128)(2,1)}, bf16[128,2048]{1,0:T(8,128)(2,1)}, u32[]{:S(2)}, u32[]{:S(2)}) collective-permute-start(bf16[128,2048]{1,0:T(8,128)(2,1)} %bitcast.148), channel_id=1, source_target_pairs={{2,0},{3,1},{4,2},{5,3},{6,4},{7,5},{8,6},{9,7},{10,8},{11,9},{12,... | collective-permute-start | bytes 1572872 | tf_op jit(solution)/shard_map/ppermute | solution.py:18
  163.8 1.1 fusion.6
  165.0 1.8 copy.121
  166.8 4.5 %fusion = bf16[1,128,2048]{2,1,0:T(8,128)(2,1)} fusion(bf16[128,1024]{0,1:T(8,128)(2,1)S(1)} %bitcast.156, bf16[2048,1024]{1,0:T(8,128)(2,1)} %all-gather.2.cloned.1.call-done), kind=kOutput, calls=%fused_computation.5 | convolution fusion | flops 537133056 | bytes 4980736 | tf_op jit(solution)/shard_map/dot_general | solution.py:85
  171.3 1.3 collective-permute-done.7
  172.6 2.4 collective-permute-done.6
  175.0 18.3 %collective-permute-done.5 = bf16[128,2048]{1,0:T(8,128)(2,1)} collective-permute-done((bf16[128,2048]{1,0:T(8,128)(2,1)}, bf16[128,2048]{1,0:T(8,128)(2,1)}, u32[]{:S(2)}, u32[]{:S(2)}) %collective-permute-start.5) | collective-permute-done | bytes 524320 | tf_op jit(solution)/shard_map/ppermute | solution.py:18
  193.3 15.7 %collective-permute-done.4 = bf16[128,2048]{1,0:T(8,128)(2,1)} collective-permute-done((bf16[128,2048]{1,0:T(8,128)(2,1)}, bf16[128,2048]{1,0:T(8,128)(2,1)}, u32[]{:S(2)}, u32[]{:S(2)}) %collective-permute-start.4) | collective-permute-done | bytes 524320 | tf_op jit(solution)/shard_map/ppermute | solution.py:18
  209.0 2.0 fusion.11
  211.8 1.1 copy.153
  213.0 165.6 %all-reduce.1 = f32[128,1024]{0,1:T(8,128)S(1)} all-reduce(bf16[128,1024]{0,1:T(8,128)(2,1)S(1)} %copy.153), channel_id=1, replica_groups=mesh['fsdp'=16,'ctx'=32] {'ctx'}, use_global_device_ids=true, to_apply=%region_3.4 | all-reduce | flops 131072 | bytes 786432 | tf_op jit(solution)/shard_map/psum | solution.py:153
  378.6 1.0 copy.122
  (44 shorter events, 6.8 us)
Async XLA Ops:
  7.2 93.7 %copy-start = (bf16[1,128,2048]{2,1,0:T(8,128)(2,1)S(1)}, bf16[1,128,2048]{2,1,0:T(8,128)(2,1)}, u32[]{:S(2)}) copy-start(bf16[1,128,2048]{2,1,0:T(8,128)(2,1)} %param.9) | copy-start | bytes 1572868
  7.2 93.6 %all-gather.2.cloned.1.call-start = ((), (), s32[]{:S(2)}) async-start(), calls=%async_computation.1 | async-start | bytes 4456448 | tf_op jit(solution)/shard_map/all_gather | solution.py:84
  7.9 203.9 %reduce-scatter.4.cloned.1.call-start = ((), (), s32[]{:S(2)}) async-start(), calls=%async_computation.2 | async-start | bytes 4456448
  8.0 51.9 %copy-start.6 = (bf16[1,128,1024]{2,1,0:T(8,128)(2,1)S(1)}, bf16[1,128,1024]{2,1,0:T(8,128)(2,1)}, u32[]{:S(2)}) copy-start(bf16[1,128,1024]{2,1,0:T(8,128)(2,1)} %param.8) | copy-start | bytes 786436
  8.0 51.8 %copy-start.7 = (bf16[1,128,1024]{2,1,0:T(8,128)(2,1)S(1)}, bf16[1,128,1024]{2,1,0:T(8,128)(2,1)}, u32[]{:S(2)}) copy-start(bf16[1,128,1024]{2,1,0:T(8,128)(2,1)} %param.7) | copy-start | bytes 786436
  9.1 39.1 %collective-permute-start = (bf16[128,2048]{1,0:T(8,128)(2,1)S(1)}, bf16[128,2048]{1,0:T(8,128)(2,1)}, u32[]{:S(2)}, u32[]{:S(2)}) collective-permute-start(bf16[128,2048]{1,0:T(8,128)(2,1)S(1)} %pad_maximum_fusion.1), channel_id=1, source_target_pairs={{30,0},{31,1},{0,2},{1,3},{2,4},{3,5},{4,6},{5,7},{6,8},{7,9},{8,1... | collective-permute-start | bytes 1572872 | tf_op jit(solution)/shard_map/ppermute | solution.py:18
  15.2 42.7 %collective-permute-start.1 = (bf16[128,2048]{1,0:T(8,128)(2,1)S(1)}, bf16[128,2048]{1,0:T(8,128)(2,1)}, u32[]{:S(2)}, u32[]{:S(2)}) collective-permute-start(bf16[128,2048]{1,0:T(8,128)(2,1)S(1)} %pad_maximum_fusion.1), channel_id=1, source_target_pairs={{31,0},{0,1},{1,2},{2,3},{3,4},{4,5},{5,6},{6,7},{7,8},{8,9},{9,10... | collective-permute-start | bytes 1572872 | tf_op jit(solution)/shard_map/ppermute | solution.py:18
  19.5 50.6 %collective-permute-start.2 = (bf16[128,2048]{1,0:T(8,128)(2,1)S(1)}, bf16[128,2048]{1,0:T(8,128)(2,1)S(1)}, u32[]{:S(2)}, u32[]{:S(2)}) collective-permute-start(bf16[128,2048]{1,0:T(8,128)(2,1)S(1)} %pad_maximum_fusion.1), channel_id=1, source_target_pairs={{1,0},{2,1},{3,2},{4,3},{5,4},{6,5},{7,6},{8,7},{9,8},{10,9},{11,1... | collective-permute-start | bytes 1572872 | tf_op jit(solution)/shard_map/ppermute | solution.py:18
  26.7 63.5 %collective-permute-start.3 = (bf16[128,2048]{1,0:T(8,128)(2,1)S(1)}, bf16[128,2048]{1,0:T(8,128)(2,1)S(1)}, u32[]{:S(2)}, u32[]{:S(2)}) collective-permute-start(bf16[128,2048]{1,0:T(8,128)(2,1)S(1)} %pad_maximum_fusion.1), channel_id=1, source_target_pairs={{2,0},{3,1},{4,2},{5,3},{6,4},{7,5},{8,6},{9,7},{10,8},{11,9},{12,... | collective-permute-start | bytes 1572872 | tf_op jit(solution)/shard_map/ppermute | solution.py:18
  33.7 65.0 %copy-start.8 = (bf16[128,8,128,1]{0,2,3,1:T(8,128)(2,1)}, bf16[128,8,128,1]{0,2,3,1:T(8,128)(2,1)S(1)}, u32[]{:S(2)}) copy-start(bf16[128,8,128,1]{0,2,3,1:T(8,128)(2,1)S(1)} %copy.137) | copy-start | bytes 786436
  95.0 2.4 copy-start.4
  117.1 1.2 copy-start.1
  118.4 0.9 copy-start.9
  119.3 1.0 copy-start.2
  143.1 29.5 %collective-permute-start.7 = (bf16[128,2048]{1,0:T(8,128)(2,1)}, bf16[128,2048]{1,0:T(8,128)(2,1)S(1)}, u32[]{:S(2)}, u32[]{:S(2)}) collective-permute-start(bf16[128,2048]{1,0:T(8,128)(2,1)} %bitcast.145), channel_id=1, source_target_pairs={{30,0},{31,1},{0,2},{1,3},{2,4},{3,5},{4,6},{5,7},{6,8},{7,9},{8,1... | collective-permute-start | bytes 1572872 | tf_op jit(solution)/shard_map/ppermute | solution.py:18
  145.0 18.8 %copy-start.3 = (bf16[8,128,4,128]{1,3,2,0:T(8,128)(2,1)S(1)}, bf16[8,128,4,128]{1,3,2,0:T(8,128)(2,1)}, u32[]{:S(2)}) copy-start(bf16[8,128,4,128]{1,3,2,0:T(8,128)(2,1)} %copy-done.2) | copy-start | bytes 3145732
  145.0 18.8 %copy-start.5 = (bf16[1,4,128,1024]{2,3,1,0:T(8,128)(2,1)S(1)}, bf16[1,4,128,1024]{2,3,1,0:T(8,128)(2,1)}, u32[]{:S(2)}) copy-start(bf16[1,4,128,1024]{2,3,1,0:T(8,128)(2,1)} %copy.106) | copy-start | bytes 3145732
  146.1 28.8 %collective-permute-start.6 = (bf16[128,2048]{1,0:T(8,128)(2,1)}, bf16[128,2048]{1,0:T(8,128)(2,1)}, u32[]{:S(2)}, u32[]{:S(2)}) collective-permute-start(bf16[128,2048]{1,0:T(8,128)(2,1)} %bitcast.146), channel_id=1, source_target_pairs={{31,0},{0,1},{1,2},{2,3},{3,4},{4,5},{5,6},{6,7},{7,8},{8,9},{9,10... | collective-permute-start | bytes 1572872 | tf_op jit(solution)/shard_map/ppermute | solution.py:18
  149.2 44.1 %collective-permute-start.5 = (bf16[128,2048]{1,0:T(8,128)(2,1)}, bf16[128,2048]{1,0:T(8,128)(2,1)}, u32[]{:S(2)}, u32[]{:S(2)}) collective-permute-start(bf16[128,2048]{1,0:T(8,128)(2,1)} %bitcast.147), channel_id=1, source_target_pairs={{1,0},{2,1},{3,2},{4,3},{5,4},{6,5},{7,6},{8,7},{9,8},{10,9},{11,1... | collective-permute-start | bytes 1572872 | tf_op jit(solution)/shard_map/ppermute | solution.py:18
  158.4 50.6 %collective-permute-start.4 = (bf16[128,2048]{1,0:T(8,128)(2,1)}, bf16[128,2048]{1,0:T(8,128)(2,1)}, u32[]{:S(2)}, u32[]{:S(2)}) collective-permute-start(bf16[128,2048]{1,0:T(8,128)(2,1)} %bitcast.148), channel_id=1, source_target_pairs={{2,0},{3,1},{4,2},{5,3},{6,4},{7,5},{8,6},{9,7},{10,8},{11,9},{12,... | collective-permute-start | bytes 1572872 | tf_op jit(solution)/shard_map/ppermute | solution.py:18
Sparse Core Ops, SparseCore 0:
  10.2 80.4 all-gather.1
  116.5 94.4 reduce-scatter.3
where the time goes:
time: 387 us; the launch traced here: 386 us
  blocking collectives  166 us (43%)
  waiting for transfers between devices  89.4 us (23%)
  starting transfers between devices  39.8 us (10%)
  local copies, waits for them, and re-layouts  39.5 us (10%)
  matrix products  27 us (7%)
  between operations  14.4 us (4%)
  other arithmetic  10.8 us (3%)
    psum x1, blocking collectives, body(): full_sum = lax.psum(fsdp_sum, 'ctx')  166 us
    ppermute x8, waiting for transfers between devices, shifted(): return lax.ppermute(block, axis, route)  88.7 us
    ppermute x8, starting transfers between devices, shifted(): return lax.ppermute(block, axis, route)  39.8 us
    unnamed x34, local copies, waits for them, and re-layouts  23.1 us
    dot_general x1, matrix products, body(): jnp.dot(placement, slot_grads.reshape(slot_total, block_rows * 2 * featur...  9.95 us
  transfers between devices with their start and end apart: 10, of which 8 were waited for; matrix products, arithmetic and copies ran while one was open for 15% of the time, Pallas kernels for 0%

commit v1 on v0

v1 whole, which is shorter than its diff:
```python
import math

import jax
import jax.numpy as jnp
from jax import lax
from jax.experimental import pallas as pl
from jax.experimental.pallas import tpu as pltpu
from jax.sharding import PartitionSpec as P

MESH = pl.DeviceIdType.MESH
F32 = jnp.float32
BF16 = jnp.bfloat16

HEADS = 8
HDIM = 128
BS = 128
HW = 1024
D = 2048
CHUNKS = 2
CW = HW // CHUNKS
CHEADS = HEADS // CHUNKS
NF = 16
NC = 32
NZ = 8
NY = 4
SCALE = HDIM**-0.5
DEAD = -1e30
HALF = BS // 2
K, V, Q, G = range(4)
OWN = 4
OFFSETS = (-1, -2, 1, 2, 0)
RING = 2 * 2 * 4 * CHUNKS


def dot_nn(a, b):
    return lax.dot_general(a, b, (((1,), (0,)), ((), ())), preferred_element_type=F32)


def dot_nt(a, b):
    return lax.dot_general(a, b, (((1,), (1,)), ((), ())), preferred_element_type=F32)


def dot_tn(a, b):
    return lax.dot_general(a, b, (((0,), (0,)), ((), ())), preferred_element_type=F32)


def kernel(
    nb_ref, q_ref, k_ref, v_ref, og_ref, w_ref,
    out_ref, qg_ref, kg_ref, vg_ref, wg_ref,
    win, relay_buf, wall, att, attall, ogall, probs, stat, statw, ar1, ar2, ar3, arsrc, arsum,
    ring_s, ring_r, relay_s, relay_r, ag_s, ag_r, a2a_s, a2a_r, st_s, st_r,
    ar1_s, ar1_r, ar2_s, ar2_r, ar3_s, ar3_r,
):
    f = lax.axis_index("fsdp")
    c = lax.axis_index("ctx")
    y, x, core = f // 8, (f // 2) % 4, f % 2
    yh, z = c // NZ, c % NZ

    def fs(yy, xx, kk):
        return yy * 8 + xx * 2 + kk

    xp, xm, x2 = (x + 1) % 4, (x + 3) % 4, (x + 2) % 4
    sib = (fs(y, x, 1 - core), c)
    ynb = (fs(1 - y, x, core), c)
    right = (fs(y, xp, core), c)
    left = (fs(y, xm, core), c)
    cnext = ((c + 1) % NC, (c + NC - 1) % NC)

    def copy(src, dst, ss, rs, dev):
        return pltpu.make_async_remote_copy(
            src_ref=src, dst_ref=dst, send_sem=ss, recv_sem=rs, device_id=dev, device_id_type=MESH
        )

    barrier = pltpu.get_barrier_semaphore()

    def greet(dev):
        pl.semaphore_signal(barrier, inc=1, device_id=dev, device_id_type=MESH)

    for d in range(1, NF):
        greet(((f + d) % NF, c))
    for d in range(1, NZ):
        greet((f, yh * NZ + (z + d) % NZ))
    for d in range(1, NY):
        greet((f, (yh + d) % NY * NZ + z))
    for d in (1, 2, NC - 2, NC - 1):
        greet((f, (c + d) % NC))
    pl.semaphore_wait(barrier, NF - 1 + NZ - 1 + NY - 1 + 4)

    source = {K: k_ref, V: v_ref, Q: q_ref}

    def cols(chunk):
        return pl.ds(chunk * CW, CW)

    def ring_index(item, chunk, way, hop):
        return ((item * CHUNKS + chunk) * 2 + way) * 2 + hop

    def ring_dst(item, chunk, way, hop):
        return win.at[item, 2 * way + hop, :, cols(chunk)]

    def ring_src(item, chunk, way, hop):
        if hop == 1:
            return win.at[item, 2 * way, :, cols(chunk)]
        if item == G:
            return win.at[item, OWN, :, cols(chunk)]
        return source[item].at[:, cols(chunk)]

    wrap_z = (NZ - 1, 0)

    def ring_send(item, chunk, hop):
        for way in range(2):
            i = ring_index(item, chunk, way, hop)
            src, dst = ring_src(item, chunk, way, hop), ring_dst(item, chunk, way, hop)
            dev = (f, cnext[way])

            @pl.when(z != wrap_z[way])
            def _():
                copy(src, dst, ring_s.at[i], ring_r.at[i], dev).start()

            @pl.when(z == wrap_z[way])
            def _():
                lo, hi = pl.ds(0, HALF), pl.ds(HALF, HALF)
                copy(src.at[lo], dst.at[lo], ring_s.at[i], ring_r.at[i], dev).start()
                copy(
                    src.at[hi], relay_buf.at[i], ring_s.at[i], relay_r.at[i], (f, yh * NZ + (NZ - 1 - z))
                ).start()

    def relay_copy(item, chunk, way, hop):
        i = ring_index(item, chunk, way, hop)
        dst = ring_dst(item, chunk, way, hop).at[pl.ds(HALF, HALF)]
        to = (f, (yh + (1 if way == 0 else NY - 1)) % NY * NZ + z)
        return copy(relay_buf.at[i], dst, relay_s.at[i], ring_r.at[i], to)

    def relay(item, chunk, hop):
        for way in range(2):
            i = ring_index(item, chunk, way, hop)

            @pl.when(z == wrap_z[1 - way])
            def _():
                copy(relay_buf.at[i], relay_buf.at[i], relay_s.at[i], relay_r.at[i], sib).wait_recv()
                relay_copy(item, chunk, way, hop).start()

    def ring_wait(item, chunk, hop):
        for way in range(2):
            i = ring_index(item, chunk, way, hop)
            dst = ring_dst(item, chunk, way, hop)
            copy(dst, dst, ring_s.at[i], ring_r.at[i], sib).wait_recv()

    def ring_step(items, hop, forward):
        for item, chunk in items:
            relay(item, chunk, hop)
        for item, chunk in items:
            ring_wait(item, chunk, hop)
            if forward:
                ring_send(item, chunk, hop + 1)

    lo, hi, full = pl.ds(0, HALF), pl.ds(HALF, HALF), pl.ds(0, BS)

    class Gather:
        def __init__(self, number, src, dst, width):
            self.n, self.src, self.dst, self.width = number, src, dst, width

        def block(self, yy, xx, kk, part=full):
            row = pl.multiple_of(fs(yy, xx, kk) * BS, BS) + part.start
            return self.dst.at[pl.ds(pl.multiple_of(row, HALF), part.size), self.width]

        def send(self, i, src, dst, dev):
            copy(src, dst, ag_s.at[self.n, i], ag_r.at[self.n, i], dev).start()

        def got(self, i, ref):
            copy(ref, ref, ag_s.at[self.n, i], ag_r.at[self.n, i], sib).wait_recv()

        def sent(self):
            sizes = {5: HALF, 6: HALF, 7: HALF, 8: HALF}
            for i in range(17):
                ref = self.block(0, 0, 0, pl.ds(0, sizes.get(i, BS)))
                copy(ref, ref, ag_s.at[self.n, i], ag_r.at[self.n, i], sib).wait_send()

        def first(self):
            mine = self.block(y, x, core)
            self.send(0, self.src, mine, ynb)
            self.send(1, self.src, mine, right)
            self.send(2, self.src, mine, left)
            self.send(9, self.src, mine, sib)

        def second(self):
            ref = self.block(1 - y, x, core)
            self.got(0, ref)
            self.send(3, ref, ref, right)
            self.send(4, ref, ref, left)
            self.send(10, ref, ref, sib)

        def third(self, far):
            yy = 1 - y if far else y
            a, b = (3, 4) if far else (1, 2)
            ha, hb = (7, 8) if far else (5, 6)
            sa, sb = (13, 14) if far else (11, 12)
            ref = self.block(yy, xm, core)
            self.got(a, ref)
            part = self.block(yy, xm, core, lo)
            self.send(ha, part, part, right)
            self.send(sa, ref, ref, sib)
            ref = self.block(yy, xp, core)
            self.got(b, ref)
            part = self.block(yy, xp, core, hi)
            self.send(hb, part, part, left)
            self.send(sb, ref, ref, sib)

        def fourth(self, far):
            yy = 1 - y if far else y
            ha, hb = (7, 8) if far else (5, 6)
            s = 16 if far else 15
            self.got(ha, self.block(yy, x2, core, lo))
            self.got(hb, self.block(yy, x2, core, hi))
            ref = self.block(yy, x2, core)
            self.send(s, ref, ref, sib)

        def last(self):
            for i in range(9, 17):
                self.got(i, self.block(0, 0, 0))

    gather_w = Gather(0, w_ref, wall, pl.ds(0, HW))
    gather_a = [Gather(1 + ch, att.at[:, cols(ch)], attall, cols(ch)) for ch in range(CHUNKS)]

    def own_att(ch):
        mine = pl.ds(pl.multiple_of(f * BS, BS), BS)
        attall[mine, cols(ch)] = att[:, cols(ch)]

    lane_block = lax.broadcasted_iota(jnp.int32, (1, 5 * BS), 1) // BS

    def mask_row(row_of, name_of):
        row = jnp.zeros((1, 5 * BS), F32)
        for s, off in enumerate(OFFSETS):
            r, name = row_of(off), name_of(off)
            live = nb_ref[r, 0] == name
            for n in range(1, 4):
                live = live | (nb_ref[r, n] == name)
            row = jnp.where(lane_block == s, jnp.where(live, 0.0, DEAD), row)
        return row

    lane = lax.broadcasted_iota(jnp.int32, (BS, BS), 1)

    def head_cols(h):
        return pl.ds(pl.multiple_of(h * HDIM, HDIM), HDIM)

    def window(item, h):
        return win[item, :, :, head_cols(h)].reshape(5 * BS, HDIM)

    def forward(ch, bias):
        def one(h, acc):
            s = dot_nt(q_ref[:, head_cols(h)], window(K, h)) * SCALE + bias
            m = jnp.max(s, axis=1, keepdims=True)
            e = jnp.exp(s - m)
            total = jnp.sum(e, axis=1, keepdims=True)
            p = e * (1.0 / total)
            probs[h] = p
            att[:, head_cols(h)] = dot_nn(p.astype(BF16), window(V, h)).astype(BF16)
            return jnp.where(lane == h, m + jnp.log(total), acc)

        stat[...] = lax.fori_loop(ch * CHEADS, (ch + 1) * CHEADS, one, stat[...])

    def backward_queries():
        def one(h, acc):
            g = win[G, OWN, :, head_cols(h)]
            delta = jnp.sum(
                g.astype(F32) * att[:, head_cols(h)].astype(F32), axis=1, keepdims=True
            )
            dp = dot_nt(g, window(V, h))
            ds = (probs[h] * (dp - delta) * SCALE).astype(BF16)
            qg_ref[:, head_cols(h)] = dot_nn(ds, window(K, h)).astype(BF16)
            return jnp.where(lane == h + HEADS, delta, acc)

        stat[...] = lax.fori_loop(0, HEADS, one, stat[...])

    def backward_keys(ch, bias):
        def one(h, _):
            row = lambda r: jnp.concatenate(
                [statw[s, pl.ds(r, 1), :] for s in range(5)], axis=1
            )
            q, g = window(Q, h), window(G, h)
            st = dot_nt(k_ref[:, head_cols(h)], q) * SCALE + bias
            pt = jnp.exp(st - row(h))
            dpt = dot_nt(v_ref[:, head_cols(h)], g)
            dst = (pt * (dpt - row(h + HEADS)) * SCALE).astype(BF16)
            vg_ref[:, head_cols(h)] = dot_nn(pt.astype(BF16), g).astype(BF16)
            kg_ref[:, head_cols(h)] = dot_nn(dst, q).astype(BF16)
            return 0

        lax.fori_loop(ch * CHEADS, (ch + 1) * CHEADS, one, 0)

    def zdev(d):
        return (f, yh * NZ + (z + d) % NZ)

    def ydev(d):
        return (f, (yh + d) % NY * NZ + z)

    AR = BS // NZ
    my_rows = pl.ds(pl.multiple_of(z * AR, AR), AR)

    def ar1_copy(ch, d):
        rows = pl.ds(pl.multiple_of((z + d) % NZ * AR, AR), AR)
        return copy(
            arsrc.at[ch, rows], ar1.at[ch, d - 1], ar1_s.at[ch, d - 1], ar1_r.at[ch, d - 1], zdev(d)
        )

    def ar2_copy(ch, d):
        return copy(
            ar2.at[ch, yh], ar2.at[ch, yh], ar2_s.at[ch, d - 1], ar2_r.at[ch, d - 1], ydev(d)
        )

    def ar3_copy(ch, d):
        return copy(
            ar3.at[ch, my_rows], ar3.at[ch, my_rows], ar3_s.at[ch, d - 1], ar3_r.at[ch, d - 1], zdev(d)
        )

    def reduce_first(ch):
        part = dot_tn(ogall[...], attall[:, cols(ch)])
        arsum[ch] = part
        arsrc[ch] = part.astype(BF16)
        for d in range(1, NZ):
            ar1_copy(ch, d).start()

    def reduce_second(ch):
        total = arsum[ch, my_rows]
        for d in range(1, NZ):
            ar1_copy(ch, d).wait_recv()
            total = total + ar1[ch, d - 1].astype(F32)
        ar2[ch, yh] = total.astype(BF16)
        for d in range(1, NY):
            ar2_copy(ch, d).start()

    def reduce_third(ch):
        for d in range(1, NY):
            ar2_copy(ch, d).wait_recv()
        total = ar2[ch, 0].astype(F32)
        for i in range(1, NY):
            total = total + ar2[ch, i].astype(F32)
        ar3[ch, my_rows] = (total * (1.0 / math.sqrt(NF * NC * BS))).astype(BF16)
        for d in range(1, NZ):
            ar3_copy(ch, d).start()

    def reduce_last(ch):
        for d in range(1, NZ):
            ar3_copy(ch, d).wait_recv()
        wg_ref[:, cols(ch)] = ar3[ch].astype(F32)

    def a2a_copy(d):
        to = (f + d) % NF
        return copy(
            og_ref.at[:, pl.ds(pl.multiple_of(to * BS, BS), BS)],
            ogall.at[pl.ds(pl.multiple_of(f * BS, BS), BS)],
            a2a_s.at[d - 1], a2a_r.at[d - 1], (to, c),
        )

    def stat_copy(s):
        return copy(
            statw.at[OWN], statw.at[s], st_s.at[s], st_r.at[s], (f, (c - OFFSETS[s] + NC) % NC)
        )

    for item, ch in ((K, 0), (V, 0), (K, 1), (V, 1)):
        ring_send(item, ch, 0)
    gather_w.first()
    wall[pl.ds(pl.multiple_of(f * BS, BS), BS), :] = w_ref[...]
    for item in (K, V, Q):
        win[item, OWN] = source[item][...]
    ogall[pl.ds(pl.multiple_of(f * BS, BS), BS), :] = og_ref[:, pl.ds(pl.multiple_of(f * BS, BS), BS)]
    stat[...] = jnp.zeros((BS, BS), F32)
    bias_q = mask_row(lambda off: c, lambda off: (c + off + NC) % NC)
    bias_k = mask_row(lambda off: (c + off + NC) % NC, lambda off: c)

    ring_step([(K, 0), (V, 0)], 0, True)
    gather_w.second()
    gather_w.third(False)
    ring_step([(K, 1), (V, 1)], 0, True)
    for ch in range(CHUNKS):
        ring_send(Q, ch, 0)
    gather_w.third(True)
    ring_step([(K, 0), (V, 0)], 1, False)
    forward(0, bias_q)
    gather_a[0].first()
    own_att(0)
    gather_w.fourth(False)
    gather_w.fourth(True)
    gather_w.last()
    for ch in range(CHUNKS):
        win[G, OWN, :, cols(ch)] = dot_nn(og_ref[...], wall[:, cols(ch)]).astype(BF16)
    for d in range(1, NF):
        a2a_copy(d).start()
    gather_a[0].second()
    ring_step([(K, 1), (V, 1)], 1, False)
    forward(1, bias_q)
    gather_a[1].first()
    own_att(1)
    ring_step([(Q, 0), (Q, 1)], 0, True)
    for ch in range(CHUNKS):
        ring_send(G, ch, 0)
    gather_a[0].third(False)
    backward_queries()
    statw[OWN] = stat[...].T[0 : 2 * HEADS]
    for s in range(4):
        stat_copy(s).start()
    gather_a[0].third(True)
    gather_a[1].second()
    gather_a[1].third(False)
    gather_a[0].fourth(False)
    gather_a[0].fourth(True)
    gather_a[0].last()
    for d in range(1, NF):
        a2a_copy(d).wait_recv()
    reduce_first(0)
    ring_step([(Q, 0), (Q, 1)], 1, False)
    gather_a[1].third(True)
    ring_step([(G, 0), (G, 1)], 0, True)
    gather_a[1].fourth(False)
    gather_a[1].fourth(True)
    gather_a[1].last()
    reduce_first(1)
    reduce_second(0)
    for i in range(4):
        rows = pl.ds(i * (D // 4), D // 4)
        out_ref[:, rows] = dot_nt(att[...], wall[rows, :]).astype(BF16)
    reduce_third(0)
    reduce_second(1)
    for s in range(4):
        stat_copy(s).wait_recv()
    ring_step([(G, 0)], 1, False)
    backward_keys(0, bias_k)
    reduce_third(1)
    ring_step([(G, 1)], 1, False)
    backward_keys(1, bias_k)
    for ch in range(CHUNKS):
        reduce_last(ch)

    for item in (K, V, Q, G):
        for ch in range(CHUNKS):
            for hop in range(2):
                for way in range(2):
                    i = ring_index(item, ch, way, hop)
                    dst = ring_dst(item, ch, way, hop)
                    copy(dst, dst, ring_s.at[i], ring_r.at[i], sib).wait_send()

                    @pl.when(z == wrap_z[1 - way])
                    def _():
                        relay_copy(item, ch, way, hop).wait_send()

    gather_w.sent()
    for ch in range(CHUNKS):
        gather_a[ch].sent()
        for d in range(1, NZ):
            ar1_copy(ch, d).wait_send()
            ar3_copy(ch, d).wait_send()
        for d in range(1, NY):
            ar2_copy(ch, d).wait_send()
    for d in range(1, NF):
        a2a_copy(d).wait_send()
    for s in range(4):
        stat_copy(s).wait_send()


def body(queries, keys, values, out_grad, weight, neighbours):
    vmem = pl.BlockSpec(memory_space=pltpu.VMEM)
    dma = pltpu.SemaphoreType.DMA
    outs = pl.pallas_call(
        kernel,
        name="layer",
        out_shape=(
            jax.ShapeDtypeStruct((BS, D), BF16),
            jax.ShapeDtypeStruct((BS, HW), BF16),
            jax.ShapeDtypeStruct((BS, HW), BF16),
            jax.ShapeDtypeStruct((BS, HW), BF16),
            jax.ShapeDtypeStruct((BS, HW), F32),
        ),
        in_specs=[pl.BlockSpec(memory_space=pltpu.SMEM)] + [vmem] * 5,
        out_specs=[vmem] * 5,
        scratch_shapes=[
            pltpu.VMEM((4, 5, BS, HW), BF16),
            pltpu.VMEM((RING, HALF, CW), BF16),
            pltpu.VMEM((D, HW), BF16),
            pltpu.VMEM((BS, HW), BF16),
            pltpu.VMEM((NF * BS, HW), BF16),
            pltpu.VMEM((NF * BS, BS), BF16),
            pltpu.VMEM((HEADS, BS, 5 * BS), F32),
            pltpu.VMEM((BS, BS), F32),
            pltpu.VMEM((5, 2 * HEADS, BS), F32),
            pltpu.VMEM((CHUNKS, NZ - 1, BS // NZ, CW), BF16),
            pltpu.VMEM((CHUNKS, NY, BS // NZ, CW), BF16),
            pltpu.VMEM((CHUNKS, BS, CW), BF16),
            pltpu.VMEM((CHUNKS, BS, CW), BF16),
            pltpu.VMEM((CHUNKS, BS, CW), F32),
            dma((RING,)), dma((RING,)), dma((RING,)), dma((RING,)),
            dma((1 + CHUNKS, 17)), dma((1 + CHUNKS, 17)),
            dma((NF - 1,)), dma((NF - 1,)),
            dma((4,)), dma((4,)),
            dma((CHUNKS, NZ - 1)), dma((CHUNKS, NZ - 1)),
            dma((CHUNKS, NY - 1)), dma((CHUNKS, NY - 1)),
            dma((CHUNKS, NZ - 1)), dma((CHUNKS, NZ - 1)),
        ],
        compiler_params=pltpu.CompilerParams(
            collective_id=0, has_side_effects=True, vmem_limit_bytes=48 * 2**20
        ),
        cost_estimate=pl.CostEstimate(
            flops=3 * 10**9, bytes_accessed=8 * 2**20, transcendentals=2 * 10**6
        ),
    )(neighbours[0], queries[0], keys[0], values[0], out_grad[0], weight)
    return (outs[0][None], outs[1][None], outs[2][None], outs[3][None], outs[4])


def solution(mesh):
    rows = P("fsdp", "ctx", None)
    return jax.shard_map(
        body,
        mesh=mesh,
        in_specs=(rows, rows, rows, rows, P("fsdp", None), P("fsdp", None, None)),
        out_specs=(rows, rows, rows, rows, P("fsdp", None)),
        check_vma=False,
    )
```

time: 387 us -> 139 us (0.36)
  the two profiles are of different devices: /device:TPU:8 before, /device:TPU:1 now
where the time goes in v1:
time: 139 us; the launch traced here: 138 us
  Pallas kernels  128 us (92%)
  local copies, waits for them, and re-layouts  9.3 us (7%)
    pallas_call x1, Pallas kernels, body(): pl.pallas_call(kernel, name='layer', out_shape=(jax.ShapeDtypeStruct((BS,...  128 us
    unnamed x17, local copies, waits for them, and re-layouts  9.21 us

profile of v1, /device:TPU:1, one launch (start us, length us, event | category | flops | bytes accessed | tf_op | source)
XLA Modules:
  0.0 137.7 jit_solution(15226797225952308540)
XLA Ops:
  0.6 0.0 copy-start.5
  0.6 0.7 copy-done.5
  1.3 0.1 copy.11.nb_ref
  1.4 0.0 copy-start
  1.4 1.0 copy-done
  2.4 0.0 copy-start.1
  2.4 0.9 copy-done.1
  3.4 0.0 copy-start.2
  3.4 0.9 copy-done.2
  4.3 0.0 copy-start.3
  4.3 0.9 copy-done.3
  5.3 0.0 copy-start.4
  5.3 0.9 copy-done.4
  6.2 127.7 %layer.1 = (bf16[128,2048]{1,0:T(8,128)(2,1)S(1)}, bf16[128,1024]{1,0:T(8,128)(2,1)S(1)}, bf16[128,1024]{1,0:T(8,128)(2,1)S(1)}, bf16[128,1024]{1,0:T(8,128)(2,1)S(1)}, f32[128,1024]{1,0:T(8,128)S(1)}) custom-call(s32[32,4]{1,0:T(8,128)S(1)} %copy.11.nb_ref, bf16[128,1024]{1,0:T(8,128)(2,1)S(1)} %bitcast.14, bf16[128,1024]{1,0:T(8,128)(2,1)S(1)} %bitcast.15, ...), custom_call_target="tpu_custom_call" | custom-call | flops 3000000000 | bytes 8388608 | tf_op jit(solution)/shard_map/layer/pallas_call | solution.py:462
  134.0 0.8 copy.17
  134.8 0.7 copy.18
  135.5 0.7 copy.19
  136.2 0.7 copy.20
  136.9 0.8 copy.21
Async XLA Ops:
  0.6 0.7 copy-start.5
  1.4 1.0 copy-start
  2.4 0.9 copy-start.1
  3.4 0.9 copy-start.2
  4.3 0.9 copy-start.3
  5.3 0.9 copy-start.4

commit v2 on v1

v2 whole, which is shorter than its diff:
```python
import math

import jax
import jax.numpy as jnp
from jax import lax
from jax.experimental import pallas as pl
from jax.experimental.pallas import tpu as pltpu
from jax.sharding import PartitionSpec as P

MESH = pl.DeviceIdType.MESH
F32 = jnp.float32
BF16 = jnp.bfloat16

HEADS = 8
HDIM = 128
BS = 128
HW = 1024
D = 2048
CHUNKS = 2
CW = HW // CHUNKS
CHEADS = HEADS // CHUNKS
NF = 16
NC = 32
NZ = 8
NY = 4
SCALE = HDIM**-0.5
DEAD = -1e30
HALF = BS // 2
K, V, Q, G = range(4)
OWN = 4
OFFSETS = (-1, -2, 1, 2, 0)
RING = 2 * 2 * 4 * CHUNKS


def dot_nn(a, b):
    return lax.dot_general(a, b, (((1,), (0,)), ((), ())), preferred_element_type=F32)


def dot_nt(a, b):
    return lax.dot_general(a, b, (((1,), (1,)), ((), ())), preferred_element_type=F32)


def dot_tn(a, b):
    return lax.dot_general(a, b, (((0,), (0,)), ((), ())), preferred_element_type=F32)


def kernel(
    nb_in, q_in, k_in, v_in, og_in, w_in,
    out_hbm, qg_hbm, kg_hbm, vg_hbm, wg_hbm,
    nb_ref, out_ref, qg_ref, kg_ref, vg_ref, wg_ref,
    win, relay_buf, og, wall, att, attall, ogall, probs, stat, statw, ar1, ar2, ar3, arsrc, ar2src, arsum,
    in_s, out_s, ring_s, ring_r, relay_s, relay_r, ag_s, ag_r, a2a_s, a2a_r, st_s, st_r,
    ar1_s, ar1_r, ar2_s, ar2_r, ar3_s, ar3_r,
):
    f = lax.axis_index("fsdp")
    c = lax.axis_index("ctx")
    y, x, core = f // 8, (f // 2) % 4, f % 2
    yh, z = c // NZ, c % NZ

    def fs(yy, xx, kk):
        return yy * 8 + xx * 2 + kk

    xp, xm, x2 = (x + 1) % 4, (x + 3) % 4, (x + 2) % 4
    sib = (fs(y, x, 1 - core), c)
    ynb = (fs(1 - y, x, core), c)
    right = (fs(y, xp, core), c)
    left = (fs(y, xm, core), c)
    ycross = (fs(1 - y, x, core), (yh + jnp.where(y == 1, 1, NY - 1)) % NY * NZ + z)

    def copy(src, dst, ss, rs, dev):
        return pltpu.make_async_remote_copy(
            src_ref=src, dst_ref=dst, send_sem=ss, recv_sem=rs, device_id=dev, device_id_type=MESH
        )

    my_w = pl.ds(pl.multiple_of(f * BS, BS), BS)
    arguments = [
        pltpu.make_async_copy(src, dst, in_s.at[i])
        for i, (src, dst) in enumerate(
            (
                (k_in, win.at[K, OWN]),
                (v_in, win.at[V, OWN]),
                (w_in, wall.at[my_w]),
                (q_in, win.at[Q, OWN]),
                (og_in, og),
                (nb_in, nb_ref),
            )
        )
    ]
    for argument in arguments:
        argument.start()

    barrier = pltpu.get_barrier_semaphore()

    def greet(dev):
        pl.semaphore_signal(barrier, inc=1, device_id=dev, device_id_type=MESH)

    mine8 = x * 2 + core
    ymine = yh * 2 + y

    def xdev(d):
        return (y * 8 + (mine8 + d) % 8, c)

    def ydev(d):
        to = (ymine + d) % 8
        return (fs(to % 2, x, core), to // 2 * NZ + z)

    def zdev(d):
        return (f, yh * NZ + (z + d) % NZ)

    for d in range(1, 8):
        greet(xdev(d))
        greet(ydev(d))
        greet(zdev(d))
    for d in (1, 2, NC - 2, NC - 1):
        greet((f, (c + d) % NC))
    pl.semaphore_wait(barrier, 3 * 7 + 4)

    def cols(chunk):
        return pl.ds(chunk * CW, CW)

    def ring_index(item, chunk, way, hop):
        return ((item * CHUNKS + chunk) * 2 + way) * 2 + hop

    def ring_dst(item, chunk, way, hop):
        return win.at[item, 2 * way + hop, :, cols(chunk)]

    def ring_src(item, chunk, way, hop):
        if hop == 1:
            return win.at[item, 2 * way, :, cols(chunk)]
        return win.at[item, OWN, :, cols(chunk)]

    wrap_z = (NZ - 1, 0)

    near = jnp.where(z == 0, 1, 0)
    NEAR, FAR = near, 1 - near

    def ring_send(item, chunk, way, hop):
        i = ring_index(item, chunk, way, hop)
        src, dst = ring_src(item, chunk, way, hop), ring_dst(item, chunk, way, hop)
        dev = (f, (c + NC + 1 - 2 * way) % NC)
        leaves = z == (NZ - 1) * (1 - way)

        @pl.when(jnp.logical_not(leaves))
        def _():
            copy(src, dst, ring_s.at[0], ring_r.at[i], dev).start()

        @pl.when(leaves)
        def _():
            lo, hi = pl.ds(0, HALF), pl.ds(HALF, HALF)
            j = relay_index(item, chunk, hop)
            copy(src.at[hi], relay_buf.at[j], ring_s.at[0], relay_r.at[j], (f, yh * NZ + (NZ - 1 - z))).start()
            copy(src.at[lo], dst.at[lo], ring_s.at[0], ring_r.at[i], dev).start()

    def relay_index(item, chunk, hop):
        return (item * CHUNKS + chunk) * 2 + hop

    def relay_copy(item, chunk, way, hop):
        i, j = ring_index(item, chunk, way, hop), relay_index(item, chunk, hop)
        dst = ring_dst(item, chunk, way, hop).at[pl.ds(HALF, HALF)]
        to = (f, (yh + (1 if way == 0 else NY - 1)) % NY * NZ + z)
        return copy(relay_buf.at[j], dst, relay_s.at[0], ring_r.at[i], to)

    def relay(item, chunk, hop):
        for way in range(2):
            j = relay_index(item, chunk, hop)

            @pl.when(z == wrap_z[1 - way])
            def _():
                copy(relay_buf.at[j], relay_buf.at[j], relay_s.at[0], relay_r.at[j], sib).wait_recv()
                relay_copy(item, chunk, way, hop).start()

    def ring_wait(item, chunk, way, hop):
        i = ring_index(item, chunk, way, hop)
        dst = ring_dst(item, chunk, way, hop)
        copy(dst, dst, ring_s.at[0], ring_r.at[i], sib).wait_recv()

    def relays(items, hop):
        for item, chunk in items:
            relay(item, chunk, hop)

    def ring_take(items, hop, ways, forward):
        for item, chunk in items:
            for way in ways:
                ring_wait(item, chunk, way, hop)
                if forward:
                    ring_send(item, chunk, way, hop + 1)

    lo, hi, full = pl.ds(0, HALF), pl.ds(HALF, HALF), pl.ds(0, BS)

    class Gather:
        def __init__(self, number, src, dst, width, one_y):
            self.n, self.src, self.dst, self.width = number, src, dst, width
            self.one_y = one_y

        def block(self, yy, xx, kk, part=full):
            yy = 0 if self.one_y else yy
            row = pl.multiple_of(fs(yy, xx, kk) * BS, BS) + part.start
            return self.dst.at[pl.ds(pl.multiple_of(row, HALF), part.size), self.width]

        def send(self, i, src, dst, dev):
            copy(src, dst, ag_s.at[self.n], ag_r.at[self.n, i], dev).start()

        def got(self, i, ref):
            copy(ref, ref, ag_s.at[self.n], ag_r.at[self.n, i], sib).wait_recv()

        def first(self):
            mine = self.block(y, x, core)
            if not self.one_y:
                self.send(0, self.src.at[lo], self.block(y, x, core, lo), ynb)
                self.send(0, self.src.at[hi], self.block(y, x, core, hi), ycross)
            self.send(1, self.src, mine, right)
            self.send(2, self.src, mine, left)
            self.send(7, self.src, mine, sib)

        def second(self):
            ref = self.block(1 - y, x, core)
            self.got(0, ref)
            self.send(3, ref, ref, right)
            self.send(4, ref, ref, left)
            self.send(7, ref, ref, sib)

        def third(self, far):
            yy = 1 - y if far else y
            a, b = (3, 4) if far else (1, 2)
            h = 6 if far else 5
            ref = self.block(yy, xm, core)
            self.got(a, ref)
            part = self.block(yy, xm, core, lo)
            self.send(h, part, part, right)
            self.send(7, ref, ref, sib)
            ref = self.block(yy, xp, core)
            self.got(b, ref)
            part = self.block(yy, xp, core, hi)
            self.send(h, part, part, left)
            self.send(7, ref, ref, sib)

        def fourth(self, far):
            ref = self.block(1 - y if far else y, x2, core)
            self.got(6 if far else 5, ref)
            self.send(7, ref, ref, sib)

        def last(self):
            self.got(7, self.dst.at[pl.ds(0, (4 if self.one_y else 8) * BS), self.width])

    gather_w = Gather(0, wall.at[my_w], wall, pl.ds(0, HW), False)
    gather_a = [
        Gather(1 + ch, att.at[:, cols(ch)], attall, cols(ch), True) for ch in range(CHUNKS)
    ]
    my_tokens = pl.ds(pl.multiple_of(mine8 * BS, BS), BS)

    def own_att(ch):
        attall[my_tokens, cols(ch)] = att[:, cols(ch)]

    lane_block = lax.broadcasted_iota(jnp.int32, (1, 5 * BS), 1) // BS

    def mask_row(row_of, name_of):
        row = jnp.zeros((1, 5 * BS), F32)
        for s, off in enumerate(OFFSETS):
            r, name = row_of(off), name_of(off)
            live = nb_ref[0, r] == name
            for n in range(1, 4):
                live = live | (nb_ref[n, r] == name)
            row = jnp.where(lane_block == s, jnp.where(live, 0.0, DEAD), row)
        return row

    lane = lax.broadcasted_iota(jnp.int32, (BS, BS), 1)

    def head_cols(h):
        return pl.ds(pl.multiple_of(h * HDIM, HDIM), HDIM)

    def window(item, h):
        return win[item, :, :, head_cols(h)].reshape(5 * BS, HDIM)

    def forward(ch, bias):
        def one(h, acc):
            s = dot_nt(win[Q, OWN, :, head_cols(h)], window(K, h)) * SCALE + bias
            m = jnp.max(s, axis=1, keepdims=True)
            e = jnp.exp(s - m)
            total = jnp.sum(e, axis=1, keepdims=True)
            p = e * (1.0 / total)
            probs[h] = p
            att[:, head_cols(h)] = dot_nn(p.astype(BF16), window(V, h)).astype(BF16)
            return jnp.where(lane == h, m + jnp.log(total), acc)

        stat[...] = lax.fori_loop(ch * CHEADS, (ch + 1) * CHEADS, one, stat[...])

    def backward_queries():
        def one(h, acc):
            g = win[G, OWN, :, head_cols(h)]
            delta = jnp.sum(
                g.astype(F32) * att[:, head_cols(h)].astype(F32), axis=1, keepdims=True
            )
            dp = dot_nt(g, window(V, h))
            ds = (probs[h] * (dp - delta) * SCALE).astype(BF16)
            qg_ref[:, head_cols(h)] = dot_nn(ds, window(K, h)).astype(BF16)
            return jnp.where(lane == h + HEADS, delta, acc)

        stat[...] = lax.fori_loop(0, HEADS, one, stat[...])

    def backward_keys(ch, bias):
        def one(h, _):
            row = lambda r: jnp.concatenate(
                [statw[s, pl.ds(r, 1), :] for s in range(5)], axis=1
            )
            q, g = window(Q, h), window(G, h)
            st = dot_nt(win[K, OWN, :, head_cols(h)], q) * SCALE + bias
            pt = jnp.exp(st - row(h))
            dpt = dot_nt(win[V, OWN, :, head_cols(h)], g)
            dst = (pt * (dpt - row(h + HEADS)) * SCALE).astype(BF16)
            vg_ref[:, head_cols(h)] = dot_nn(pt.astype(BF16), g).astype(BF16)
            kg_ref[:, head_cols(h)] = dot_nn(dst, q).astype(BF16)
            return 0

        lax.fori_loop(ch * CHEADS, (ch + 1) * CHEADS, one, 0)

    AR = BS // NZ
    my_rows = pl.ds(pl.multiple_of(z * AR, AR), AR)

    def ar1_copy(ch, d):
        rows = pl.ds(pl.multiple_of((z + d) % NZ * AR, AR), AR)
        return copy(
            arsrc.at[ch, :, rows], ar1.at[ch, d - 1], ar1_s.at[ch], ar1_r.at[ch], zdev(d)
        )

    def ar2_copy(ch, d):
        return copy(
            ar2src.at[ch, (ymine + d) % 2], ar2.at[ch, ymine], ar2_s.at[ch], ar2_r.at[ch], ydev(d)
        )

    def ar3_copy(ch, d):
        return copy(
            ar3.at[ch, my_rows], ar3.at[ch, my_rows], ar3_s.at[ch], ar3_r.at[ch], zdev(d)
        )

    def arrived(ref, sem):
        copy(ref, ref, sem, sem, sib).wait_recv()

    def reduce_first(ch):
        part = dot_tn(ogall[...], attall[:, cols(ch)]).reshape(2, BS, CW)
        arsum[ch] = part
        arsrc[ch] = part.astype(BF16)
        for d in range(1, NZ):
            ar1_copy(ch, d).start()

    def reduce_second(ch):
        total = arsum[ch, :, my_rows]
        arrived(ar1.at[ch], ar1_r.at[ch])
        for d in range(1, NZ):
            total = total + ar1[ch, d - 1].astype(F32)
        ar2src[ch] = total.astype(BF16)
        ar2[ch, ymine] = ar2src[ch, y]
        for d in range(1, 8):
            ar2_copy(ch, d).start()

    def reduce_third(ch):
        arrived(ar2.at[ch, 0:7], ar2_r.at[ch])
        total = ar2[ch, 0].astype(F32)
        for i in range(1, 8):
            total = total + ar2[ch, i].astype(F32)
        ar3[ch, my_rows] = (total * (1.0 / math.sqrt(NF * NC * BS))).astype(BF16)
        for d in range(1, NZ):
            ar3_copy(ch, d).start()

    def reduce_last(ch):
        arrived(ar3.at[ch, pl.ds(0, 7 * AR)], ar3_r.at[ch])
        wg_ref[:, cols(ch)] = ar3[ch].astype(F32)

    def a2a_copy(d, yl):
        to = (mine8 + d) % 8
        return copy(
            og.at[:, pl.ds(pl.multiple_of((yl * 8 + to) * BS, BS), BS)],
            ogall.at[my_tokens, pl.ds(yl * BS, BS)],
            a2a_s.at[0], a2a_r.at[0], xdev(d),
        )

    results = [
        (out_ref, out_hbm), (qg_ref, qg_hbm), (kg_ref, kg_hbm), (vg_ref, vg_hbm), (wg_ref, wg_hbm)
    ]

    def result_copy(i, ch):
        src, dst = results[i]
        half = src.shape[1] // CHUNKS
        part = pl.ds(ch * half, half)
        return pltpu.make_async_copy(src.at[:, part], dst.at[:, part], out_s.at[i, ch])

    def stat_copy(s):
        return copy(
            statw.at[OWN], statw.at[s], st_s.at[0], st_r.at[0], (f, (c - OFFSETS[s] + NC) % NC)
        )

    KV0, KV1 = [(K, 0), (V, 0)], [(K, 1), (V, 1)]
    QS, GS = [(Q, 0), (Q, 1)], [(G, 0), (G, 1)]
    BOTH = (NEAR, FAR)
    arguments[0].wait()
    arguments[1].wait()
    for item, ch in KV0:
        for way in BOTH:
            ring_send(item, ch, way, 0)
    arguments[2].wait()
    gather_w.first()
    for item, ch in KV1:
        for way in BOTH:
            ring_send(item, ch, way, 0)
    arguments[3].wait()
    arguments[4].wait()
    for d in range(1, 8):
        for yl in range(2):
            a2a_copy(d, yl).start()
    arguments[5].wait()
    for yl in range(2):
        ogall[my_tokens, pl.ds(yl * BS, BS)] = og[:, pl.ds(pl.multiple_of((yl * 8 + mine8) * BS, BS), BS)]
    stat[...] = jnp.zeros((BS, BS), F32)
    bias_q = mask_row(lambda off: c, lambda off: (c + off + NC) % NC)
    bias_k = mask_row(lambda off: (c + off + NC) % NC, lambda off: c)

    relays(KV0, 0)
    ring_take(KV0, 0, (NEAR,), True)
    gather_w.third(False)
    relays(KV1, 0)
    ring_take(KV1, 0, (NEAR,), True)
    ring_take(KV0, 0, (FAR,), True)
    gather_w.second()
    relays(KV0, 1)
    ring_take(KV1, 0, (FAR,), True)
    for item, ch in QS:
        for way in BOTH:
            ring_send(item, ch, way, 0)
    gather_w.third(True)
    relays(KV1, 1)
    ring_take(KV0, 1, BOTH, False)
    forward(0, bias_q)
    gather_a[0].first()
    own_att(0)
    relays(QS, 0)
    ring_take(QS, 0, (NEAR,), True)
    gather_w.fourth(False)
    gather_w.fourth(True)
    ring_take(KV1, 1, BOTH, False)
    forward(1, bias_q)
    gather_a[1].first()
    own_att(1)
    gather_a[0].third(False)
    gather_w.last()
    for ch in range(CHUNKS):
        win[G, OWN, :, cols(ch)] = dot_nn(og[...], wall[:, cols(ch)]).astype(BF16)
    for item, ch in GS:
        for way in BOTH:
            ring_send(item, ch, way, 0)
    ring_take(QS, 0, (FAR,), True)
    gather_a[0].fourth(False)
    relays(QS, 1)
    gather_a[1].third(False)
    backward_queries()
    statw[OWN] = stat[...].T[0 : 2 * HEADS]
    for s in range(4):
        stat_copy(s).start()
    result_copy(1, 0).start()
    result_copy(1, 1).start()
    gather_a[0].last()
    arrived(ogall.at[pl.ds(0, 7 * BS)], a2a_r.at[0])
    reduce_first(0)
    ring_take(GS, 0, (NEAR,), True)
    gather_a[1].fourth(False)
    relays(GS, 0)
    gather_a[1].last()
    reduce_first(1)
    for i in range(4):
        rows = pl.ds(i * (D // 4), D // 4)
        out_ref[:, rows] = dot_nt(att[...], wall[rows, :]).astype(BF16)
    result_copy(0, 0).start()
    result_copy(0, 1).start()
    ring_take(GS, 0, (FAR,), True)
    reduce_second(0)
    relays(GS, 1)
    reduce_second(1)
    ring_take(QS, 1, BOTH, False)
    arrived(statw.at[0:4], st_r.at[0])
    reduce_third(0)
    reduce_third(1)
    ring_take(GS[:1], 1, BOTH, False)
    backward_keys(0, bias_k)
    result_copy(2, 0).start()
    result_copy(3, 0).start()
    ring_take(GS[1:], 1, BOTH, False)
    backward_keys(1, bias_k)
    result_copy(2, 1).start()
    result_copy(3, 1).start()
    for ch in range(CHUNKS):
        reduce_last(ch)
        result_copy(4, ch).start()

    def all_sent(ref, sem):
        copy(ref, ref, sem, sem, sib).wait_send()

    all_sent(win.at[:, 0:4], ring_s.at[0])

    @pl.when((z == 0) | (z == NZ - 1))
    def _():
        all_sent(relay_buf, relay_s.at[0])

    all_sent(wall.at[pl.ds(0, 15 * BS)], ag_s.at[0])
    for ch in range(CHUNKS):
        all_sent(attall.at[pl.ds(0, 7 * BS), cols(ch)], ag_s.at[1 + ch])
        all_sent(ar1.at[ch], ar1_s.at[ch])
        all_sent(ar2.at[ch, 0:7], ar2_s.at[ch])
        all_sent(ar3.at[ch, pl.ds(0, 7 * AR)], ar3_s.at[ch])
    all_sent(ogall.at[pl.ds(0, 7 * BS)], a2a_s.at[0])
    all_sent(statw.at[0:4], st_s.at[0])
    for i in range(5):
        for ch in range(CHUNKS):
            result_copy(i, ch).wait()


def hand_over(*refs):
    ins, outs, held, in_s, out_s = refs[:5], refs[5:10], refs[10:15], refs[15], refs[16]
    come = [pltpu.make_async_copy(ins[i], held[i], in_s.at[i]) for i in range(5)]
    go = [pltpu.make_async_copy(held[i], outs[i], out_s.at[i]) for i in range(5)]
    for copy in come:
        copy.start()
    for i in range(5):
        come[i].wait()
        go[i].start()
    for copy in go:
        copy.wait()


def body(queries, keys, values, out_grad, weight, neighbours):
    dma = pltpu.SemaphoreType.DMA
    outs = pl.pallas_call(
        kernel,
        name="layer",
        out_shape=(
            jax.ShapeDtypeStruct((BS, D), BF16),
            jax.ShapeDtypeStruct((BS, HW), BF16),
            jax.ShapeDtypeStruct((BS, HW), BF16),
            jax.ShapeDtypeStruct((BS, HW), BF16),
            jax.ShapeDtypeStruct((BS, HW), F32),
        ),
        in_specs=[pl.BlockSpec(memory_space=pl.ANY)] * 6,
        out_specs=[pl.BlockSpec(memory_space=pl.ANY)] * 5,
        scratch_shapes=[
            pltpu.SMEM((4, NC), jnp.int32),
            pltpu.VMEM((BS, D), BF16),
            pltpu.VMEM((BS, HW), BF16),
            pltpu.VMEM((BS, HW), BF16),
            pltpu.VMEM((BS, HW), BF16),
            pltpu.VMEM((BS, HW), F32),
            pltpu.VMEM((4, 5, BS, HW), BF16),
            pltpu.VMEM((RING // 2, HALF, CW), BF16),
            pltpu.VMEM((BS, D), BF16),
            pltpu.VMEM((D, HW), BF16),
            pltpu.VMEM((BS, HW), BF16),
            pltpu.VMEM((8 * BS, HW), BF16),
            pltpu.VMEM((8 * BS, 2 * BS), BF16),
            pltpu.VMEM((HEADS, BS, 5 * BS), F32),
            pltpu.VMEM((BS, BS), F32),
            pltpu.VMEM((5, 2 * HEADS, BS), F32),
            pltpu.VMEM((CHUNKS, NZ - 1, 2, BS // NZ, CW), BF16),
            pltpu.VMEM((CHUNKS, 8, BS // NZ, CW), BF16),
            pltpu.VMEM((CHUNKS, BS, CW), BF16),
            pltpu.VMEM((CHUNKS, 2, BS, CW), BF16),
            pltpu.VMEM((CHUNKS, 2, BS // NZ, CW), BF16),
            pltpu.VMEM((CHUNKS, 2, BS, CW), F32),
            dma((6,)), dma((5, CHUNKS)),
            dma((1,)), dma((RING,)), dma((1,)), dma((RING // 2,)),
            dma((1 + CHUNKS,)), dma((1 + CHUNKS, 8)),
            dma((1,)), dma((1,)),
            dma((1,)), dma((1,)),
            dma((CHUNKS,)), dma((CHUNKS,)),
            dma((CHUNKS,)), dma((CHUNKS,)),
            dma((CHUNKS,)), dma((CHUNKS,)),
        ],
        compiler_params=pltpu.CompilerParams(
            collective_id=0, has_side_effects=True, vmem_limit_bytes=62 * 2**20
        ),
        cost_estimate=pl.CostEstimate(
            flops=3 * 10**9, bytes_accessed=8 * 2**20, transcendentals=2 * 10**6
        ),
    )(neighbours[0].T, queries[0], keys[0], values[0], out_grad[0], weight)
    placed = pl.pallas_call(
        hand_over,
        name="hand_over",
        out_shape=tuple(jax.ShapeDtypeStruct(o.shape, o.dtype) for o in outs),
        in_specs=[pl.BlockSpec(memory_space=pl.ANY)] * 5,
        out_specs=[pl.BlockSpec(memory_space=pl.ANY)] * 5,
        scratch_shapes=[pltpu.VMEM(o.shape, o.dtype) for o in outs] + [dma((5,)), dma((5,))],
        cost_estimate=pl.CostEstimate(flops=0, bytes_accessed=4 * 2**20, transcendentals=0),
    )(*outs)
    return (placed[0][None], placed[1][None], placed[2][None], placed[3][None], placed[4])


def solution(mesh):
    rows = P("fsdp", "ctx", None)
    return jax.shard_map(
        body,
        mesh=mesh,
        in_specs=(rows, rows, rows, rows, P("fsdp", None), P("fsdp", None, None)),
        out_specs=(rows, rows, rows, rows, P("fsdp", None)),
        check_vma=False,
    )
```

time: 139 us -> 92.6 us (0.67)
  Pallas kernels: 128 us -> 91.8 us
  local copies, waits for them, and re-layouts: 9.3 us -> 0 us
    pallas_call x1, Pallas kernels: 128 us -> 89.4 us  [body(): pl.pallas_call(kernel, name='layer', out_shape=(jax.ShapeDtypeStruct((BS,...]
    unnamed x17 -> x0, local copies, waits for them, and re-layouts: 9.21 us -> none
    pallas_call x0 -> x1, Pallas kernels: none -> 2.35 us  [body(): pl.pallas_call(hand_over, name='hand_over', out_shape=tuple((jax.ShapeDty...]
where the time goes in v2:
time: 92.6 us; the launch traced here: 92.4 us
  Pallas kernels  91.8 us (99%)
    pallas_call x1, Pallas kernels, body(): pl.pallas_call(kernel, name='layer', out_shape=(jax.ShapeDtypeStruct((BS,...  89.4 us
    pallas_call x1, Pallas kernels, body(): pl.pallas_call(hand_over, name='hand_over', out_shape=tuple((jax.ShapeDty...  2.35 us

profile of v2, /device:TPU:1, one launch (start us, length us, event | category | flops | bytes accessed | tf_op | source)
XLA Modules:
  0.0 92.4 jit_solution(3628419491849528566)
XLA Ops:
  0.6 89.4 %layer.1 = (bf16[128,2048]{1,0:T(8,128)(2,1)}, bf16[128,1024]{1,0:T(8,128)(2,1)}, bf16[128,1024]{1,0:T(8,128)(2,1)}, bf16[128,1024]{1,0:T(8,128)(2,1)}, f32[128,1024]{1,0:T(8,128)}) custom-call(s32[4,32]{1,0:T(4,128)} %bitcast.19, bf16[128,1024]{1,0:T(8,128)(2,1)} %bitcast.13, bf16[128,1024]{1,0:T(8,128)(2,1)} %bitcast.14, bf16[128,1024]{1,0:T(8,128)(2,1)} %bitcast.15, ...), custom_call_target="tpu_custom_call" | custom-call | flops 3000000000 | bytes 8388608 | tf_op jit(solution)/shard_map/layer/pallas_call | solution.py:529
  90.1 2.4 %hand_over.1 = (bf16[128,2048]{1,0:T(8,128)(2,1)}, bf16[128,1024]{1,0:T(8,128)(2,1)}, bf16[128,1024]{1,0:T(8,128)(2,1)}, bf16[128,1024]{1,0:T(8,128)(2,1)}, f32[128,1024]{1,0:T(8,128)}) custom-call(bf16[128,2048]{1,0:T(8,128)(2,1)} %get-tuple-element.15.refs_0_, bf16[128,1024]{1,0:T(8,128)(2,1)} %get-tuple-element.16.refs_1_, ...), custom_call_target="tpu_custom_call" | custom-call | bytes 4194304 | tf_op jit(solution)/shard_map/hand_over/pallas_call | solution.py:580

commit v3 on v2

--- a/solution.py
+++ b/solution.py
@@ -48,9 +48,9 @@
     nb_in, q_in, k_in, v_in, og_in, w_in,
     out_hbm, qg_hbm, kg_hbm, vg_hbm, wg_hbm,
     nb_ref, out_ref, qg_ref, kg_ref, vg_ref, wg_ref,
-    win, relay_buf, og, wall, att, attall, ogall, probs, stat, statw, ar1, ar2, ar3, arsrc, ar2src, arsum,
+    win, relay_buf, og, wall, att, attall, ogall, probs, stat, statw, arother, arx, ar1, ar2, ar3, arsrc, arsum,
     in_s, out_s, ring_s, ring_r, relay_s, relay_r, ag_s, ag_r, a2a_s, a2a_r, st_s, st_r,
-    ar1_s, ar1_r, ar2_s, ar2_r, ar3_s, ar3_r,
+    ar0_s, ar0_r, ar1_s, ar1_r, ar2_s, ar2_r, ar3_s, ar3_r,
 ):
     f = lax.axis_index("fsdp")
     c = lax.axis_index("ctx")
@@ -133,6 +133,7 @@
 
     near = jnp.where(z == 0, 1, 0)
     NEAR, FAR = near, 1 - near
+    inner = (z != 0) & (z != NZ - 1)
 
     def ring_send(item, chunk, way, hop):
         i = ring_index(item, chunk, way, hop)
@@ -282,7 +283,7 @@
             att[:, head_cols(h)] = dot_nn(p.astype(BF16), window(V, h)).astype(BF16)
             return jnp.where(lane == h, m + jnp.log(total), acc)
 
-        stat[...] = lax.fori_loop(ch * CHEADS, (ch + 1) * CHEADS, one, stat[...])
+        stat[...] = lax.fori_loop(ch * CHEADS, (ch + 1) * CHEADS, one, stat[...], unroll=True)
 
     def backward_queries():
         def one(h, acc):
@@ -295,7 +296,7 @@
             qg_ref[:, head_cols(h)] = dot_nn(ds, window(K, h)).astype(BF16)
             return jnp.where(lane == h + HEADS, delta, acc)
 
-        stat[...] = lax.fori_loop(0, HEADS, one, stat[...])
+        stat[...] = lax.fori_loop(0, HEADS, one, stat[...], unroll=True)
 
     def backward_keys(ch, bias):
         def one(h, _):
@@ -311,58 +312,65 @@
             kg_ref[:, head_cols(h)] = dot_nn(dst, q).astype(BF16)
             return 0
 
-        lax.fori_loop(ch * CHEADS, (ch + 1) * CHEADS, one, 0)
+        lax.fori_loop(ch * CHEADS, (ch + 1) * CHEADS, one, 0, unroll=True)
 
     AR = BS // NZ
     my_rows = pl.ds(pl.multiple_of(z * AR, AR), AR)
 
+    def y_copy(ch, part, dev):
+        return copy(arother.at[ch, part], arx.at[ch, part], ar0_s.at[ch], ar0_r.at[ch], dev)
+
     def ar1_copy(ch, d):
         rows = pl.ds(pl.multiple_of((z + d) % NZ * AR, AR), AR)
-        return copy(
-            arsrc.at[ch, :, rows], ar1.at[ch, d - 1], ar1_s.at[ch], ar1_r.at[ch], zdev(d)
-        )
+        return copy(arsrc.at[ch, rows], ar1.at[ch, d - 1], ar1_s.at[ch], ar1_r.at[ch], zdev(d))
 
     def ar2_copy(ch, d):
-        return copy(
-            ar2src.at[ch, (ymine + d) % 2], ar2.at[ch, ymine], ar2_s.at[ch], ar2_r.at[ch], ydev(d)
-        )
+        to = (f, (yh + d) % NY * NZ + z)
+        return copy(ar2.at[ch, yh], ar2.at[ch, yh], ar2_s.at[ch], ar2_r.at[ch], to)
 
     def ar3_copy(ch, d):
-        return copy(
-            ar3.at[ch, my_rows], ar3.at[ch, my_rows], ar3_s.at[ch], ar3_r.at[ch], zdev(d)
-        )
+        return copy(ar3.at[ch, my_rows], ar3.at[ch, my_rows], ar3_s.at[ch], ar3_r.at[ch], zdev(d))
 
     def arrived(ref, sem):
         copy(ref, ref, sem, sem, sib).wait_recv()
 
+    def feature_rows(yl):
+        return pl.ds(pl.multiple_of(yl * BS, BS), BS)
+
+    def reduce_start(ch):
+        arother[ch] = dot_tn(ogall[:, feature_rows(1 - y)], attall[:, cols(ch)]).astype(BF16)
+        y_copy(ch, lo, ynb).start()
+        y_copy(ch, hi, ycross).start()
+        arsum[ch] = dot_tn(ogall[:, feature_rows(y)], attall[:, cols(ch)])
+
     def reduce_first(ch):
-        part = dot_tn(ogall[...], attall[:, cols(ch)]).reshape(2, BS, CW)
-        arsum[ch] = part
-        arsrc[ch] = part.astype(BF16)
+        arrived(arx.at[ch], ar0_r.at[ch])
+        total = arsum[ch] + arx[ch].astype(F32)
+        arsum[ch] = total
+        arsrc[ch] = total.astype(BF16)
         for d in range(1, NZ):
             ar1_copy(ch, d).start()
 
     def reduce_second(ch):
-        total = arsum[ch, :, my_rows]
+        total = arsum[ch, my_rows]
         arrived(ar1.at[ch], ar1_r.at[ch])
         for d in range(1, NZ):
             total = total + ar1[ch, d - 1].astype(F32)
-        ar2src[ch] = total.astype(BF16)
-        ar2[ch, ymine] = ar2src[ch, y]
-        for d in range(1, 8):
+        ar2[ch, yh] = total.astype(BF16)
+        for d in range(1, NY):
             ar2_copy(ch, d).start()
 
     def reduce_third(ch):
-        arrived(ar2.at[ch, 0:7], ar2_r.at[ch])
+        arrived(ar2.at[ch, 0 : NY - 1], ar2_r.at[ch])
         total = ar2[ch, 0].astype(F32)
-        for i in range(1, 8):
+        for i in range(1, NY):
             total = total + ar2[ch, i].astype(F32)
         ar3[ch, my_rows] = (total * (1.0 / math.sqrt(NF * NC * BS))).astype(BF16)
         for d in range(1, NZ):
             ar3_copy(ch, d).start()
 
     def reduce_last(ch):
-        arrived(ar3.at[ch, pl.ds(0, 7 * AR)], ar3_r.at[ch])
+        arrived(ar3.at[ch, pl.ds(0, (NZ - 1) * AR)], ar3_r.at[ch])
         wg_ref[:, cols(ch)] = ar3[ch].astype(F32)
 
     def a2a_copy(d, yl):
@@ -458,24 +466,37 @@
     result_copy(1, 1).start()
     gather_a[0].last()
     arrived(ogall.at[pl.ds(0, 7 * BS)], a2a_r.at[0])
+    reduce_start(0)
+
+    @pl.when(inner)
+    def _():
+        ring_take(GS, 0, (NEAR,), True)
+
+    gather_a[1].fourth(False)
+    gather_a[1].last()
+    reduce_start(1)
+
+    relays(GS, 0)
     reduce_first(0)
-    ring_take(GS, 0, (NEAR,), True)
-    gather_a[1].fourth(False)
-    relays(GS, 0)
-    gather_a[1].last()
-    reduce_first(1)
+
+    @pl.when(jnp.logical_not(inner))
+    def _():
+        ring_take(GS, 0, (NEAR,), True)
+
     for i in range(4):
         rows = pl.ds(i * (D // 4), D // 4)
         out_ref[:, rows] = dot_nt(att[...], wall[rows, :]).astype(BF16)
     result_copy(0, 0).start()
     result_copy(0, 1).start()
+    reduce_first(1)
+
     ring_take(GS, 0, (FAR,), True)
     reduce_second(0)
-    relays(GS, 1)
     reduce_second(1)
     ring_take(QS, 1, BOTH, False)
     arrived(statw.at[0:4], st_r.at[0])
     reduce_third(0)
+    relays(GS, 1)
     reduce_third(1)
     ring_take(GS[:1], 1, BOTH, False)
     backward_keys(0, bias_k)
@@ -502,7 +523,8 @@
     for ch in range(CHUNKS):
         all_sent(attall.at[pl.ds(0, 7 * BS), cols(ch)], ag_s.at[1 + ch])
         all_sent(ar1.at[ch], ar1_s.at[ch])
-        all_sent(ar2.at[ch, 0:7], ar2_s.at[ch])
+        all_sent(ar2.at[ch, 0 : NY - 1], ar2_s.at[ch])
+        all_sent(arx.at[ch], ar0_s.at[ch])
         all_sent(ar3.at[ch, pl.ds(0, 7 * AR)], ar3_s.at[ch])
     all_sent(ogall.at[pl.ds(0, 7 * BS)], a2a_s.at[0])
     all_sent(statw.at[0:4], st_s.at[0])
@@ -555,17 +577,19 @@
             pltpu.VMEM((HEADS, BS, 5 * BS), F32),
             pltpu.VMEM((BS, BS), F32),
             pltpu.VMEM((5, 2 * HEADS, BS), F32),
-            pltpu.VMEM((CHUNKS, NZ - 1, 2, BS // NZ, CW), BF16),
-            pltpu.VMEM((CHUNKS, 8, BS // NZ, CW), BF16),
             pltpu.VMEM((CHUNKS, BS, CW), BF16),
-            pltpu.VMEM((CHUNKS, 2, BS, CW), BF16),
-            pltpu.VMEM((CHUNKS, 2, BS // NZ, CW), BF16),
-            pltpu.VMEM((CHUNKS, 2, BS, CW), F32),
+            pltpu.VMEM((CHUNKS, BS, CW), BF16),
+            pltpu.VMEM((CHUNKS, NZ - 1, BS // NZ, CW), BF16),
+            pltpu.VMEM((CHUNKS, NY, BS // NZ, CW), BF16),
+            pltpu.VMEM((CHUNKS, BS, CW), BF16),
+            pltpu.VMEM((CHUNKS, BS, CW), BF16),
+            pltpu.VMEM((CHUNKS, BS, CW), F32),
             dma((6,)), dma((5, CHUNKS)),
             dma((1,)), dma((RING,)), dma((1,)), dma((RING // 2,)),
             dma((1 + CHUNKS,)), dma((1 + CHUNKS, 8)),
             dma((1,)), dma((1,)),
             dma((1,)), dma((1,)),
+            dma((CHUNKS,)), dma((CHUNKS,)),
             dma((CHUNKS,)), dma((CHUNKS,)),
             dma((CHUNKS,)), dma((CHUNKS,)),
             dma((CHUNKS,)), dma((CHUNKS,)),

time: 92.6 us -> 89.9 us (0.971)
  Pallas kernels: 91.8 us -> 89.1 us
    pallas_call x1, Pallas kernels: 89.4 us -> 86.7 us  [body(): pl.pallas_call(kernel, name='layer', out_shape=(jax.ShapeDtypeStruct((BS,...]
where the time goes in v3:
time: 89.9 us; the launch traced here: 89.7 us
  Pallas kernels  89.1 us (99%)
    pallas_call x1, Pallas kernels, body(): pl.pallas_call(kernel, name='layer', out_shape=(jax.ShapeDtypeStruct((BS,...  86.7 us
    pallas_call x1, Pallas kernels, body(): pl.pallas_call(hand_over, name='hand_over', out_shape=tuple((jax.ShapeDty...  2.35 us

profile of v3, /device:TPU:1, one launch (start us, length us, event | category | flops | bytes accessed | tf_op | source)
XLA Modules:
  0.0 89.7 jit_solution(9915264832263002212)
XLA Ops:
  0.6 86.7 %layer.1 = (bf16[128,2048]{1,0:T(8,128)(2,1)}, bf16[128,1024]{1,0:T(8,128)(2,1)}, bf16[128,1024]{1,0:T(8,128)(2,1)}, bf16[128,1024]{1,0:T(8,128)(2,1)}, f32[128,1024]{1,0:T(8,128)}) custom-call(s32[4,32]{1,0:T(4,128)} %bitcast.19, bf16[128,1024]{1,0:T(8,128)(2,1)} %bitcast.13, bf16[128,1024]{1,0:T(8,128)(2,1)} %bitcast.14, bf16[128,1024]{1,0:T(8,128)(2,1)} %bitcast.15, ...), custom_call_target="tpu_custom_call" | custom-call | flops 3000000000 | bytes 8388608 | tf_op jit(solution)/shard_map/layer/pallas_call | solution.py:551
  87.4 2.4 %hand_over.1 = (bf16[128,2048]{1,0:T(8,128)(2,1)}, bf16[128,1024]{1,0:T(8,128)(2,1)}, bf16[128,1024]{1,0:T(8,128)(2,1)}, bf16[128,1024]{1,0:T(8,128)(2,1)}, f32[128,1024]{1,0:T(8,128)}) custom-call(bf16[128,2048]{1,0:T(8,128)(2,1)} %get-tuple-element.15.refs_0_, bf16[128,1024]{1,0:T(8,128)(2,1)} %get-tuple-element.16.refs_1_, ...), custom_call_target="tpu_custom_call" | custom-call | bytes 4194304 | tf_op jit(solution)/shard_map/hand_over/pallas_call | solution.py:604

commit v4 on v3

--- a/solution.py
+++ b/solution.py
@@ -86,9 +86,6 @@
             )
         )
     ]
-    for argument in arguments:
-        argument.start()
-
     barrier = pltpu.get_barrier_semaphore()
 
     def greet(dev):
@@ -113,6 +110,8 @@
         greet(zdev(d))
     for d in (1, 2, NC - 2, NC - 1):
         greet((f, (c + d) % NC))
+    for argument in arguments:
+        argument.start()
     pl.semaphore_wait(barrier, 3 * 7 + 4)
 
     def cols(chunk):
@@ -147,10 +146,16 @@
 
         @pl.when(leaves)
         def _():
+            if by_one_way(item, hop):
+                copy(src, dst, ring_s.at[0], ring_r.at[i], dev).start()
+                return
             lo, hi = pl.ds(0, HALF), pl.ds(HALF, HALF)
             j = relay_index(item, chunk, hop)
             copy(src.at[hi], relay_buf.at[j], ring_s.at[0], relay_r.at[j], (f, yh * NZ + (NZ - 1 - z))).start()
             copy(src.at[lo], dst.at[lo], ring_s.at[0], ring_r.at[i], dev).start()
+
+    def by_one_way(item, hop):
+        return item == G and hop == 1
 
     def relay_index(item, chunk, hop):
         return (item * CHUNKS + chunk) * 2 + hop
@@ -162,6 +167,8 @@
         return copy(relay_buf.at[j], dst, relay_s.at[0], ring_r.at[i], to)
 
     def relay(item, chunk, hop):
+        if by_one_way(item, hop):
+            return
         for way in range(2):
             j = relay_index(item, chunk, hop)
 
@@ -496,7 +503,6 @@
     ring_take(QS, 1, BOTH, False)
     arrived(statw.at[0:4], st_r.at[0])
     reduce_third(0)
-    relays(GS, 1)
     reduce_third(1)
     ring_take(GS[:1], 1, BOTH, False)
     backward_keys(0, bias_k)
@@ -517,7 +523,7 @@
 
     @pl.when((z == 0) | (z == NZ - 1))
     def _():
-        all_sent(relay_buf, relay_s.at[0])
+        all_sent(relay_buf.at[pl.ds(0, 14)], relay_s.at[0])
 
     all_sent(wall.at[pl.ds(0, 15 * BS)], ag_s.at[0])
     for ch in range(CHUNKS):

time: 89.9 us -> 88.5 us (0.984)
  Pallas kernels: 89.1 us -> 87.2 us
    pallas_call x1, Pallas kernels: 86.7 us -> 84.8 us  [body(): pl.pallas_call(kernel, name='layer', out_shape=(jax.ShapeDtypeStruct((BS,...]
where the time goes in v4:
time: 88.5 us; the launch traced here: 87.8 us
  Pallas kernels  87.2 us (99%)
    pallas_call x1, Pallas kernels, body(): pl.pallas_call(kernel, name='layer', out_shape=(jax.ShapeDtypeStruct((BS,...  84.8 us
    pallas_call x1, Pallas kernels, body(): pl.pallas_call(hand_over, name='hand_over', out_shape=tuple((jax.ShapeDty...  2.35 us

profile of v4, /device:TPU:1, one launch (start us, length us, event | category | flops | bytes accessed | tf_op | source)
XLA Modules:
  0.0 87.8 jit_solution(12523151715645435065)
XLA Ops:
  0.6 84.8 %layer.1 = (bf16[128,2048]{1,0:T(8,128)(2,1)}, bf16[128,1024]{1,0:T(8,128)(2,1)}, bf16[128,1024]{1,0:T(8,128)(2,1)}, bf16[128,1024]{1,0:T(8,128)(2,1)}, f32[128,1024]{1,0:T(8,128)}) custom-call(s32[4,32]{1,0:T(4,128)} %bitcast.19, bf16[128,1024]{1,0:T(8,128)(2,1)} %bitcast.13, bf16[128,1024]{1,0:T(8,128)(2,1)} %bitcast.14, bf16[128,1024]{1,0:T(8,128)(2,1)} %bitcast.15, ...), custom_call_target="tpu_custom_call" | custom-call | flops 3000000000 | bytes 8388608 | tf_op jit(solution)/shard_map/layer/pallas_call | solution.py:557
  85.5 2.4 %hand_over.1 = (bf16[128,2048]{1,0:T(8,128)(2,1)}, bf16[128,1024]{1,0:T(8,128)(2,1)}, bf16[128,1024]{1,0:T(8,128)(2,1)}, bf16[128,1024]{1,0:T(8,128)(2,1)}, f32[128,1024]{1,0:T(8,128)}) custom-call(bf16[128,2048]{1,0:T(8,128)(2,1)} %get-tuple-element.15.refs_0_, bf16[128,1024]{1,0:T(8,128)(2,1)} %get-tuple-element.16.refs_1_, ...), custom_call_target="tpu_custom_call" | custom-call | bytes 4194304 | tf_op jit(solution)/shard_map/hand_over/pallas_call | solution.py:610

commit v5 on v4

--- a/solution.py
+++ b/solution.py
@@ -437,11 +437,11 @@
     gather_w.second()
     relays(KV0, 1)
     ring_take(KV1, 0, (FAR,), True)
+    gather_w.third(True)
+    relays(KV1, 1)
     for item, ch in QS:
         for way in BOTH:
             ring_send(item, ch, way, 0)
-    gather_w.third(True)
-    relays(KV1, 1)
     ring_take(KV0, 1, BOTH, False)
     forward(0, bias_q)
     gather_a[0].first()

time: 88.5 us -> 94.2 us (1.064)
  the two profiles are of different devices: /device:TPU:1 before, /device:TPU:24 now
where the time goes in v5:
time: 94.2 us; the launch traced here: 94 us
  Pallas kernels  93.4 us (99%)
    pallas_call x1, Pallas kernels, body(): pl.pallas_call(kernel, name='layer', out_shape=(jax.ShapeDtypeStruct((BS,...  91 us
    pallas_call x1, Pallas kernels, body(): pl.pallas_call(hand_over, name='hand_over', out_shape=tuple((jax.ShapeDty...  2.35 us

profile of v5, /device:TPU:24, one launch (start us, length us, event | category | flops | bytes accessed | tf_op | source)
XLA Modules:
  0.0 94.0 jit_solution(15842124882111799786)
XLA Ops:
  0.6 91.0 %layer.1 = (bf16[128,2048]{1,0:T(8,128)(2,1)}, bf16[128,1024]{1,0:T(8,128)(2,1)}, bf16[128,1024]{1,0:T(8,128)(2,1)}, bf16[128,1024]{1,0:T(8,128)(2,1)}, f32[128,1024]{1,0:T(8,128)}) custom-call(s32[4,32]{1,0:T(4,128)} %bitcast.19, bf16[128,1024]{1,0:T(8,128)(2,1)} %bitcast.13, bf16[128,1024]{1,0:T(8,128)(2,1)} %bitcast.14, bf16[128,1024]{1,0:T(8,128)(2,1)} %bitcast.15, ...), custom_call_target="tpu_custom_call" | custom-call | flops 3000000000 | bytes 8388608 | tf_op jit(solution)/shard_map/layer/pallas_call | solution.py:557
  91.7 2.4 %hand_over.1 = (bf16[128,2048]{1,0:T(8,128)(2,1)}, bf16[128,1024]{1,0:T(8,128)(2,1)}, bf16[128,1024]{1,0:T(8,128)(2,1)}, bf16[128,1024]{1,0:T(8,128)(2,1)}, f32[128,1024]{1,0:T(8,128)}) custom-call(bf16[128,2048]{1,0:T(8,128)(2,1)} %get-tuple-element.15.refs_0_, bf16[128,1024]{1,0:T(8,128)(2,1)} %get-tuple-element.16.refs_1_, ...), custom_call_target="tpu_custom_call" | custom-call | bytes 4194304 | tf_op jit(solution)/shard_map/hand_over/pallas_call | solution.py:610
